TPU v7x, 32 devices: a whole 2x2x4 slice. The times are simulated.
32 devices in a mesh: req: 8 (over z, y), tp: 4 (over x, core).
Axes of the slice: x: 2, y: 2, z: 4, core: 2. Of those that a mesh axis runs over, the one named last changes fastest.
Arguments:
- hidden_in: bfloat16 [2048, 2048], P('req'), may hold values from -40 to 40
- recompute_pos: int32 [8, 256], replicated, may hold values from 0 to 16383, as said below
- req_lengths: int32 [8], replicated, may hold values from 1 to 32, as said below
- stretch_order: int32 [8, 32], replicated, may hold values from 0 to 255, as said below
- page_table: int32 [2, 256], replicated, may hold values from 0 to 31, as said below
- cached_key_pool: bfloat16 [256, 512, 1024], P('req', None, 'tp'), may hold values from -6 to 6
- cached_value_pool: bfloat16 [256, 512, 1024], P('req', None, 'tp'), may hold values from -6 to 6
- attn_gain: float32 [2048], replicated, may hold values from 0.5 to 2
- w_query: bfloat16 [2048, 2048], P(None, 'tp'), may hold values from -1 to 1
- w_key: bfloat16 [2048, 1024], P(None, 'tp'), may hold values from -1 to 1
- value_weight: bfloat16 [2048, 1024], P(None, 'tp'), may hold values from -0.125 to 0.125
- query_gain: float32 [128], replicated, may hold values from 0 to 20
- key_norm_gain: float32 [128], replicated, may hold values from 0 to 20
- w_out: bfloat16 [2048, 2048], P('tp'), may hold values from -0.5 to 0.5
- ffn_gain: float32 [2048], replicated, may hold values from 0.5 to 2
- w_gate: bfloat16 [2048, 6144], P(None, 'tp'), may hold values from -0.125 to 0.125
- w_up: bfloat16 [2048, 6144], P(None, 'tp'), may hold values from -0.125 to 0.125
- w_down: bfloat16 [6144, 2048], P('tp'), may hold values from -0.078125 to 0.078125
Outputs:
- layer_out: bfloat16 [2048, 2048], P('req')
Inputs may be any that keep to these rules, and one draw needn't show every extreme that they name: `req_lengths`: on each draw, the requests of one index along req (chosen anew each time) all have 32 stretches; the others have 1 to 32. `stretch_order`: every stretch id appears exactly once over all requests and places, places at or past a request's length included. `page_table`: every slot of every index along req holds exactly one stretch id, and each index holds exactly 4 of the 32 ids listed by the requests of any one index. `recompute_pos`: strictly increasing along a request, below 512 times the request's length; every request recomputes its first and its last position.
All inputs are finite; a program needn't handle non-finite values.
Results may differ from a plain program's by a relative error of at most 0.015.
The roundings to bfloat16 on the way count: a program that leaves them out, or rounds other values in their place, can miss the bound.
Values may be sent and summed in bfloat16 or wider, within the bound.
A program may use at most 256 MiB of HBM per device.

v0:
```python
import jax
import jax.numpy as jnp
from jax import lax
from jax.sharding import PartitionSpec as P

STRETCH_TOKENS = 512
MOST_STRETCHES = 32
REQ_DEV = 1
RECOMPUTE_TOKENS = 256


eps_norm = 1e-06
rope_base = 1000000.0
floor_score = -1e30


def norm_rows(matrix, gain_vec):
    wide = matrix.astype(jnp.float32)
    factor = lax.rsqrt(jnp.mean(wide * wide, axis=-1, keepdims=True) + eps_norm)
    return wide * factor * gain_vec


def angles(position, head_size):
    half_dim = head_size // 2
    frequency = rope_base ** (-jnp.arange(half_dim, dtype=jnp.float32) / half_dim)
    return position.astype(jnp.float32)[..., None] * frequency


def rotate_halves(vector, angle_arg):
    half_dim = vector.shape[-1] // 2
    lower_half = vector[..., :half_dim]
    upper_half = vector[..., half_dim:]
    cosine = jnp.cos(angle_arg)
    sine_part = jnp.sin(angle_arg)
    return jnp.concatenate(
        [
            lower_half * cosine - upper_half * sine_part,
            upper_half * cosine + lower_half * sine_part,
        ],
        axis=-1,
    )


def rotary_heads(raw_proj, gain_vec, position, head_count):
    head_size = gain_vec.shape[0]
    split_heads = raw_proj.reshape(raw_proj.shape[0], head_count, head_size)
    normed = norm_rows(split_heads, gain_vec)
    return rotate_halves(normed, angles(position, head_size)[:, None, :]).astype(jnp.bfloat16)


def block_stats(grouped_heads, gathered_stretch_keys, values, live_mask):
    count_of_rows, key_heads, groups, head_size = grouped_heads.shape
    scores = jnp.einsum(
        "mhgd,khd->hgmk", grouped_heads, gathered_stretch_keys, preferred_element_type=jnp.float32
    ) * head_size ** (-0.5)
    row_peak = jnp.max(jnp.where(live_mask, scores, floor_score), axis=-1)
    weights = jnp.where(live_mask, jnp.exp(scores - row_peak[..., None]), 0.0)
    weight_sum = jnp.sum(weights, axis=-1)
    weighted = jnp.einsum(
        "hgmk,khd->mhgd", weights.astype(jnp.bfloat16), values, preferred_element_type=jnp.float32
    )
    head_total = key_heads * groups
    return (
        weighted.reshape(count_of_rows, head_total, head_size),
        row_peak.transpose(2, 0, 1).reshape(count_of_rows, head_total),
        weight_sum.transpose(2, 0, 1).reshape(count_of_rows, head_total),
    )


def merge_stats(weighted, row_peak, weight_sum):
    row_top = jnp.max(row_peak, axis=0)
    factor = jnp.exp(row_peak - row_top[None])
    merged = jnp.sum(weighted * factor[..., None], axis=0)
    total_sum = jnp.sum(weight_sum * factor, axis=0)
    result = (merged / total_sum[..., None]).astype(jnp.bfloat16)
    return result.reshape(result.shape[0], -1)


def swiglu(rows_in, w_gate, w_up):
    gate_proj = jnp.dot(rows_in, w_gate, preferred_element_type=jnp.float32)
    up_proj = jnp.dot(rows_in, w_up, preferred_element_type=jnp.float32)
    return (jax.nn.silu(gate_proj) * up_proj).astype(jnp.bfloat16)


def on_device(
    hidden_in,
    recompute_pos,
    req_lengths,
    stretch_order,
    page_table,
    cached_key_pool,
    cached_value_pool,
    attn_gain,
    w_query,
    w_key,
    value_weight,
    query_gain,
    key_norm_gain,
    w_out,
    ffn_gain,
    w_gate,
    w_up,
    w_down,
):
    req_count = lax.axis_size("req")
    my_index = lax.axis_index("req")
    head_size = query_gain.shape[0]
    query_heads = w_query.shape[1] // head_size
    key_heads = w_key.shape[1] // head_size
    groups = query_heads // key_heads
    count_of_rows = hidden_in.shape[0]
    local_reqs = REQ_DEV
    req_rows = RECOMPUTE_TOKENS
    entries = local_reqs * MOST_STRETCHES
    pair_cap = entries // req_count
    normed = norm_rows(hidden_in, attn_gain).astype(jnp.bfloat16)
    query_raw = jnp.dot(normed, w_query, preferred_element_type=jnp.float32)
    unnormed_keys = jnp.dot(normed, w_key, preferred_element_type=jnp.float32)
    recomputed_values = (
        jnp.dot(normed, value_weight, preferred_element_type=jnp.float32)
        .astype(jnp.bfloat16)
        .reshape(count_of_rows, key_heads, head_size)
    )
    my_positions = lax.dynamic_slice_in_dim(recompute_pos, my_index * local_reqs, local_reqs, 0)
    my_lengths = lax.dynamic_slice_in_dim(req_lengths, my_index * local_reqs, local_reqs, 0)
    flattened_position = my_positions.reshape(count_of_rows)
    queries = rotary_heads(query_raw, query_gain, flattened_position, query_heads)
    recomputed_keys = rotary_heads(unnormed_keys, key_norm_gain, flattened_position, key_heads)
    grouped_heads = queries.reshape(count_of_rows, key_heads, groups, head_size)
    row_owner = jnp.arange(count_of_rows) // req_rows
    own_mask = (row_owner[None, :] == row_owner[:, None]) & (
        flattened_position[None, :] <= flattened_position[:, None]
    )
    fresh_sum, fresh_peak, fresh_total = block_stats(
        grouped_heads, recomputed_keys, recomputed_values, own_mask
    )
    holder_table = page_table[0][stretch_order]
    slot_table = page_table[1][stretch_order]
    holder_hits = holder_table[:, :, None] == jnp.arange(req_count)[None, None, :]
    hit_counts = jnp.cumsum(holder_hits.astype(jnp.int32), axis=1)
    pair_rank = jnp.sum(jnp.where(holder_hits, hit_counts - 1, 0), axis=2)
    my_sends = (holder_table == my_index)[:, :, None] & (
        pair_rank[:, :, None] == jnp.arange(pair_cap)[None, None, :]
    )
    send_slot = jnp.sum(jnp.where(my_sends, slot_table[:, :, None], 0), axis=1)
    send_keys = cached_key_pool[send_slot]
    send_values = cached_value_pool[send_slot]
    got_keys, got_values = (
        lax.all_to_all(send_keys, "req", split_axis=0, concat_axis=0, tiled=True),
        lax.all_to_all(send_values, "req", split_axis=0, concat_axis=0, tiled=True),
    )
    my_holder = lax.dynamic_index_in_dim(holder_table, my_index, 0, keepdims=False)
    my_rank = lax.dynamic_index_in_dim(pair_rank, my_index, 0, keepdims=False)
    buffer = my_holder * pair_cap + my_rank
    position_shift_angle = angles(jnp.arange(MOST_STRETCHES) * STRETCH_TOKENS, head_size)[
        None, :, None, None, :
    ]
    gathered_stretch_keys = got_keys.reshape((req_count * pair_cap,) + got_keys.shape[2:])[buffer]
    gathered_stretch_keys = gathered_stretch_keys.reshape(
        local_reqs, MOST_STRETCHES, STRETCH_TOKENS, key_heads, head_size
    )
    gathered_stretch_keys = rotate_halves(
        gathered_stretch_keys.astype(jnp.float32), position_shift_angle
    ).astype(jnp.bfloat16)
    gathered_stretch_keys = gathered_stretch_keys.reshape(
        local_reqs, MOST_STRETCHES * STRETCH_TOKENS, key_heads, head_size
    )
    gathered_stretch_values = got_values.reshape((req_count * pair_cap,) + got_values.shape[2:])[
        buffer
    ]
    gathered_stretch_values = gathered_stretch_values.reshape(
        local_reqs, MOST_STRETCHES * STRETCH_TOKENS, key_heads, head_size
    )
    key_place = jnp.arange(MOST_STRETCHES * STRETCH_TOKENS)

    def cached_stats(packed):
        group_query, position, length, key_block, value_block = packed
        live_mask = (key_place[None, :] < position[:, None]) & (
            key_place[None, :] // STRETCH_TOKENS < length
        )
        return block_stats(group_query, key_block, value_block, live_mask)

    held_sum, held_peak, held_total = lax.map(
        cached_stats,
        (
            grouped_heads.reshape(local_reqs, req_rows, key_heads, groups, head_size),
            my_positions,
            my_lengths,
            gathered_stretch_keys,
            gathered_stretch_values,
        ),
    )
    attended = merge_stats(
        jnp.stack([held_sum.reshape(fresh_sum.shape), fresh_sum]),
        jnp.stack([held_peak.reshape(fresh_peak.shape), fresh_peak]),
        jnp.stack([held_total.reshape(fresh_total.shape), fresh_total]),
    )
    attn_out = lax.psum(
        jnp.dot(attended, w_out, preferred_element_type=jnp.float32).astype(jnp.bfloat16), "tp"
    ).astype(jnp.float32)
    residual = (hidden_in.astype(jnp.float32) + attn_out).astype(jnp.bfloat16)
    normed_ffn = norm_rows(residual, ffn_gain).astype(jnp.bfloat16)
    hidden = swiglu(normed_ffn, w_gate, w_up)
    ffn_out = lax.psum(
        jnp.dot(hidden, w_down, preferred_element_type=jnp.float32).astype(jnp.bfloat16), "tp"
    ).astype(jnp.float32)
    return (residual.astype(jnp.float32) + ffn_out).astype(jnp.bfloat16)


def solution(mesh):
    return jax.shard_map(
        on_device,
        mesh=mesh,
        in_specs=(
            P("req", None),
            P(),
            P(),
            P(),
            P(),
            P("req", None, "tp"),
            P("req", None, "tp"),
            P(),
            P(None, "tp"),
            P(None, "tp"),
            P(None, "tp"),
            P(),
            P(),
            P("tp", None),
            P(),
            P(None, "tp"),
            P(None, "tp"),
            P("tp", None),
        ),
        out_specs=P("req", None),
        check_vma=False,
    )
```

profile of v0, /device:TPU:29, one launch (start us, length us, event | category | flops | bytes accessed | tf_op | source)
XLA Modules:
  0.0 547.0 jit_solution(14144394142408173517)
XLA Ops:
  8.2 1.9 gather_fusion
  11.1 1.9 gather_fusion.1
  13.5 8.4 %gather_fusion.4 = bf16[32,512,256]{2,1,0:T(8,128)(2,1)} fusion(bf16[32,512,256]{2,1,0:T(8,128)(2,1)} %param.23, s32[1024]{0:T(1024)S(1)} %pad_clamp_fusion.1), kind=kCustom, calls=%fused_computation.4 | custom fusion | bytes 16777344 | tf_op jit(solution)/shard_map/gather | solution.py:146
  21.9 5.6 %all-to-all-start.1 = ((bf16[8,4,512,256]{3,2,1,0:T(8,128)(2,1)}), bf16[8,4,512,256]{3,2,1,0:T(8,128)(2,1)}, u32[]{:S(2)}, u32[]{:S(2)}) async-start(bf16[8,4,512,256]{3,2,1,0:T(8,128)(2,1)} %bitcast.94), calls=%async_computation.1 | async-start | bytes 16777216 | tf_op jit(solution)/shard_map/all_to_all | solution.py:149
  28.5 3.1 fusion.57
  31.6 1.2 reshape.386
  36.0 2.2 multiply_reduce_fusion.1
  38.8 1.4 select_reduce_fusion
  41.7 8.5 %gather_fusion.2 = bf16[32,512,256]{2,1,0:T(8,128)(2,1)} fusion(bf16[32,512,256]{2,1,0:T(8,128)(2,1)} %param.24, s32[1024]{0:T(1024)S(1)} %pad_clamp_fusion.1), kind=kCustom, calls=%fused_computation.2 | custom fusion | bytes 16777344 | tf_op jit(solution)/shard_map/gather | solution.py:147
  51.1 2.2 convolution_convert_fusion.2
  53.4 1.1 fusion.27
  54.5 154.5 %all-to-all-done.1 = bf16[8,4,512,256]{3,2,1,0:T(8,128)(2,1)} async-done(((bf16[8,4,512,256]{3,2,1,0:T(8,128)(2,1)}), bf16[8,4,512,256]{3,2,1,0:T(8,128)(2,1)}, u32[]{:S(2)}, u32[]{:S(2)}) %all-to-all-start.1) | async-done | bytes 8388640 | tf_op jit(solution)/shard_map/all_to_all | solution.py:149
  209.0 5.6 %all-to-all-start = ((bf16[8,4,512,256]{3,2,1,0:T(8,128)(2,1)}), bf16[8,4,512,256]{3,2,1,0:T(8,128)(2,1)}, u32[]{:S(2)}, u32[]{:S(2)}) async-start(bf16[8,4,512,256]{3,2,1,0:T(8,128)(2,1)} %bitcast.95), calls=%async_computation | async-start | bytes 16777216 | tf_op jit(solution)/shard_map/all_to_all | solution.py:150
  214.6 9.3 %fusion.8 = pred[256,16384]{0,1:T(8,128)(4,1)} fusion(s32[256]{0:T(256)S(1)} %bitcast.112, pred[16384]{0:T(1024)(128)(4,1)S(1)} %fusion.39), kind=kLoop, calls=%fused_computation.16 | loop fusion | flops 8388608 | bytes 4211712 | tf_op jit(solution)/shard_map/while/body/eval_jaxpr/and | solution.py:178
  224.0 8.4 %gather_fusion.5 = bf16[32,512,256]{2,1,0:T(8,128)(2,1)} fusion(bf16[32,512,256]{2,1,0:T(8,128)(2,1)} %bitcast.10, s32[1024]{0:T(1024)S(1)} %pad_clamp_fusion), kind=kCustom, calls=%fused_computation.5 | custom fusion | bytes 16777344 | tf_op jit(solution)/shard_map/gather | solution.py:158
  232.4 12.4 %copy.103 = f32[32,512,256]{1,2,0:T(8,128)} copy(bf16[32,512,256]{2,1,0:T(8,128)(2,1)} %gather_fusion.5) | data formatting | bytes 25165824 | tf_op jit(solution)/shard_map/convert_element_type | solution.py:163
  244.7 9.7 %subtract_convert_fusion = (bf16[1,32,512,2,64]{2,4,3,1,0:T(8,128)(2,1)}, bf16[1,32,512,2,64]{2,4,3,1,0:T(8,128)(2,1)}) fusion(f32[1,32,512,2,128]{2,4,3,1,0:T(8,128)} %bitcast.93, f32[32,64]{1,0:T(8,128)S(1)} %get-tuple-element.50, f32[32,64]{1,0:T(8,128)S(1)} %get-tuple-element.49), kind=kLoop, calls=%fused_computation.23 | loop fusion | flops 16777216 | bytes 25182208 | tf_op jit(solution)/shard_map/convert.10
  254.4 8.4 %copy.104 = bf16[1,32,512,2,64]{4,2,1,3,0:T(8,128)(2,1)} copy(bf16[1,32,512,2,64]{2,4,3,1,0:T(8,128)(2,1)} %get-tuple-element.27) | data formatting | bytes 8388608 | tf_op jit(solution)/shard_map/convert.10
  262.8 8.5 %copy.105 = bf16[1,32,512,2,64]{4,2,1,3,0:T(8,128)(2,1)} copy(bf16[1,32,512,2,64]{2,4,3,1,0:T(8,128)(2,1)} %get-tuple-element.28) | data formatting | bytes 8388608 | tf_op jit(solution)/shard_map/convert.9
  271.3 31.7 %fusion = (f32[2,2,256]{2,1,0:T(2,128)S(1)}, f32[2,16384,256,2]{2,1,3,0:T(8,128)}) fusion(pred[256,16384]{0,1:T(8,128)(4,1)} %fusion.8, bf16[256,2,2,64]{3,0,2,1:T(8,128)(2,1)S(1)} %bitcast.104, bf16[256,2,2,64]{3,0,2,1:T(8,128)(2,1)S(1)} %bitcast.102, bf16[16384,2,64]{2,0,1:T(8,128)(2,1)} %bitcast.97, bf16[16384,2,64]{2,0,1:T(8,128)(2,1)} %bitcast.96), kind=kOutput, calls=%fused_computation.8 | convolution fusion | flops 4362599424 | bytes 79958016 | tf_op jit(solution)/shard_map/while/body/eval_jaxpr/mhgd,khd->hgmk/dot_general | solution.py:53
  303.0 22.7 %fusion.3 = f32[2,2,256]{2,1,0:T(2,128)S(1)} fusion(f32[2,16384,256,2]{2,1,3,0:T(8,128)} %get-tuple-element.56, f32[2,2,256]{2,1,0:T(2,128)S(1)} %get-tuple-element.55, pred[256,16384]{0,1:T(8,128)(4,1)} %fusion.8), kind=kLoop, calls=%fused_computation.11 | loop fusion | flops 67107840 | bytes 71311360 | tf_op jit(solution)/shard_map/while/body/eval_jaxpr/reduce_sum | solution.py:58
  325.7 70.3 %all-to-all-done = bf16[8,4,512,256]{3,2,1,0:T(8,128)(2,1)} async-done(((bf16[8,4,512,256]{3,2,1,0:T(8,128)(2,1)}), bf16[8,4,512,256]{3,2,1,0:T(8,128)(2,1)}, u32[]{:S(2)}, u32[]{:S(2)}) %all-to-all-start) | async-done | bytes 8388640 | tf_op jit(solution)/shard_map/all_to_all | solution.py:150
  396.0 8.5 %gather_fusion.3 = bf16[32,512,256]{2,1,0:T(8,128)(2,1)} fusion(bf16[32,512,256]{2,1,0:T(8,128)(2,1)} %bitcast.4, s32[1024]{0:T(1024)S(1)} %pad_clamp_fusion), kind=kCustom, calls=%fused_computation.3 | custom fusion | bytes 16777344 | tf_op jit(solution)/shard_map/gather | solution.py:168
  404.5 12.5 %squeeze.29 = bf16[16384,2,128]{2,1,0:T(2,128)(2,1)} reshape(bf16[32,512,256]{2,1,0:T(8,128)(2,1)} %gather_fusion.3) | data formatting | bytes 16777216 | tf_op jit(solution)/shard_map/while/body/jit(dynamic_index_in_dim)/squeeze | solution.py:183
  417.0 27.9 %fusion.5 = f32[2,128,2,256]{3,1,2,0:T(8,128)S(1)} fusion(f32[2,16384,256,2]{2,1,3,0:T(8,128)} %get-tuple-element.56, f32[2,2,256]{2,1,0:T(2,128)S(1)} %get-tuple-element.55, pred[256,16384]{0,1:T(8,128)(4,1)} %fusion.8, bf16[16384,2,128,1]{2,1,0,3:T(2,128)(2,1)} %bitcast.98), kind=kOutput, calls=%fused_computation.13 | convolution fusion | flops 4362076160 | bytes 80220160 | tf_op jit(solution)/shard_map/while/body/eval_jaxpr/hgmk,khd->mhgd/dot_general | solution.py:59
  445.1 1.7 convolution_convert_fusion
  446.9 36.6 %all-reduce.3.cloned.1.call-done = bf16[256,2048]{1,0:T(8,128)(2,1)} async-done(((bf16[256,2048]{1,0:T(8,128)(2,1)}), bf16[256,2048]{1,0:T(8,128)(2,1)}) %all-reduce.3.cloned.1.call-update) | async-done | bytes 1048592 | tf_op jit(solution)/shard_map/psum | solution.py:198
  483.5 2.0 fusion.18
  485.6 5.8 %fusion.34 = f32[256,1536]{1,0:T(8,128)} fusion(bf16[2048,1536]{1,0:T(8,128)(2,1)} %param.33, bf16[256,2048]{1,0:T(8,128)(2,1)S(1)} %get-tuple-element.24, f32[2048]{0:T(1024)S(1)} %copy-done.9, f32[256]{0:T(256)S(1)} %add_rsqrt_fusion.2), kind=kOutput, calls=%fused_computation.62 | convolution fusion | flops 1612709888 | bytes 8922112 | tf_op jit(solution)/shard_map/dot_general | solution.py:80
  491.4 9.6 %convolution_convert_fusion.1 = bf16[256,2048]{1,0:T(8,128)(2,1)} fusion(bf16[1536,2048]{1,0:T(8,128)(2,1)} %param.35, bf16[2048,1536]{1,0:T(8,128)(2,1)} %param.34, f32[256,1536]{1,0:T(8,128)} %fusion.34, bf16[256,2048]{1,0:T(8,128)(2,1)S(1)} %get-tuple-element.24, f32[2048]{0:T(1024)S(1)} %copy-done.9, f32[256]{0:T(256)S(1)} %add_rsqrt_fusion.2), kind=kOutput, calls=%fused_computation.33 | convolution fusion | flops 3226206208 | bytes 16262144 | tf_op jit(solution)/shard_map/dot_general | solution.py:205
  501.0 36.6 %all-reduce.5.cloned.1.call-done = bf16[256,2048]{1,0:T(8,128)(2,1)} async-done(((bf16[256,2048]{1,0:T(8,128)(2,1)}), bf16[256,2048]{1,0:T(8,128)(2,1)}) %all-reduce.5.cloned.1.call-update) | async-done | bytes 1048592 | tf_op jit(solution)/shard_map/psum | solution.py:204
  537.6 2.6 fusion.21
  (77 shorter events, 10.5 us)
Async XLA Ops:
  6.5 438.6 %copy-start = (bf16[512,2048]{1,0:T(8,128)(2,1)S(1)}, bf16[512,2048]{1,0:T(8,128)(2,1)}, u32[]{:S(2)}) copy-start(bf16[512,2048]{1,0:T(8,128)(2,1)} %param.31) | copy-start | bytes 6291460
  21.9 6.3 %copy-start.1 = (bf16[256,2048]{1,0:T(8,128)(2,1)S(1)}, bf16[256,2048]{1,0:T(8,128)(2,1)}, u32[]{:S(2)}) copy-start(bf16[256,2048]{1,0:T(8,128)(2,1)} %param.18) | copy-start | bytes 3145732
  21.9 6.6 %copy-start.8 = (f32[2048]{0:T(1024)S(1)}, f32[2048]{0:T(1024)}, u32[]{:S(2)}) copy-start(f32[2048]{0:T(1024)} %param.25) | copy-start | bytes 24580
  21.9 11.9 %copy-start.6 = (f32[128]{0:T(128)S(1)}, f32[128]{0:T(128)}, u32[]{:S(2)}) copy-start(f32[128]{0:T(128)} %param.29) | copy-start | bytes 1540
  21.9 187.1 %all-to-all-start.1 = ((bf16[8,4,512,256]{3,2,1,0:T(8,128)(2,1)}), bf16[8,4,512,256]{3,2,1,0:T(8,128)(2,1)}, u32[]{:S(2)}, u32[]{:S(2)}) async-start(bf16[8,4,512,256]{3,2,1,0:T(8,128)(2,1)} %bitcast.94), calls=%async_computation.1 | async-start | bytes 16777216 | tf_op jit(solution)/shard_map/all_to_all | solution.py:149
  27.5 8.0 %copy-start.10 = (s32[8]{0:T(128)S(1)}, s32[8]{0:T(128)}, u32[]{:S(2)}) copy-start(s32[8]{0:T(128)} %param.20) | copy-start | bytes 100
  27.5 11.1 %copy-start.7 = (f32[128]{0:T(128)S(1)}, f32[128]{0:T(128)}, u32[]{:S(2)}) copy-start(f32[128]{0:T(128)} %param.30) | copy-start | bytes 1540
  209.0 187.0 %all-to-all-start = ((bf16[8,4,512,256]{3,2,1,0:T(8,128)(2,1)}), bf16[8,4,512,256]{3,2,1,0:T(8,128)(2,1)}, u32[]{:S(2)}, u32[]{:S(2)}) async-start(bf16[8,4,512,256]{3,2,1,0:T(8,128)(2,1)} %bitcast.95), calls=%async_computation | async-start | bytes 16777216 | tf_op jit(solution)/shard_map/all_to_all | solution.py:150
  214.6 268.9 %all-reduce.3.cloned.1.call-start = ((), (), s32[]{:S(2)}) async-start(), calls=%async_computation.2 | async-start | bytes 2097152 | tf_op jit(solution)/shard_map/psum | solution.py:198
  262.8 8.5 %copy-start.3 = (bf16[256,4,64]{2,0,1:T(8,128)(2,1)S(1)}, bf16[256,4,64]{2,0,1:T(8,128)(2,1)}, u32[]{:S(2)}) copy-start(bf16[256,4,64]{2,0,1:T(8,128)(2,1)} %copy.109) | copy-start | bytes 393220
  417.0 27.9 %copy-start.4 = (f32[1,256,4]{1,2,0:T(4,128)S(1)}, f32[1,256,4]{1,2,0:T(4,128)}, u32[]{:S(2)}) copy-start(f32[1,256,4]{1,2,0:T(4,128)} %stack_reshape.8) | copy-start | bytes 12292
  417.0 27.9 %copy-start.5 = (f32[1,256,4]{1,2,0:T(4,128)S(1)}, f32[1,256,4]{1,2,0:T(4,128)}, u32[]{:S(2)}) copy-start(f32[1,256,4]{1,2,0:T(4,128)} %stack.15) | copy-start | bytes 12292
  417.0 27.9 %copy-start.2 = (f32[2,128,2,256]{3,1,2,0:T(8,128)S(1)}, f32[2,128,2,256]{3,1,2,0:T(8,128)}, u32[]{:S(2)}) copy-start(f32[2,128,2,256]{3,1,2,0:T(8,128)} %fusion.27) | copy-start | bytes 1572868
  444.9 40.7 %copy-start.9 = (f32[2048]{0:T(1024)S(1)}, f32[2048]{0:T(1024)}, u32[]{:S(2)}) copy-start(f32[2048]{0:T(1024)} %param.32) | copy-start | bytes 24580
  446.8 90.8 %all-reduce.5.cloned.1.call-start = ((), (), s32[]{:S(2)}) async-start(), calls=%async_computation.3 | async-start | bytes 2097152 | tf_op jit(solution)/shard_map/psum | solution.py:204
Sparse Core Ops, SparseCore 0:
  446.9 36.5 all-reduce.2
  501.1 36.4 all-reduce.4
where the time goes:
time: 551 us; the launch traced here: 547 us
  waiting for transfers between devices  298 us (54%)
  matrix products  86.6 us (16%)
  local copies, waits for them, and re-layouts  85.4 us (15%)
  other arithmetic  52 us (9%)
  between operations  13.7 us (2%)
  starting transfers between devices  11.2 us (2%)
    all_to_all x1, waiting for transfers between devices, on_device(): lax.all_to_all(send_keys, 'req', split_axis=0, concat_axis=0, tiled=True)  155 us
    all_to_all x1, waiting for transfers between devices, on_device(): lax.all_to_all(send_values, 'req', split_axis=0, concat_axis=0, tiled=True)  70.3 us
    psum x1, waiting for transfers between devices, on_device(): lax.psum(jnp.dot(hidden, w_down, preferred_element_type=jnp.float32).asty...  36.6 us
    psum x1, waiting for transfers between devices, on_device(): lax.psum(jnp.dot(attended, w_out, preferred_element_type=jnp.float32).ast...  36.6 us
    dot_general x2, matrix products, block_stats(): jnp.einsum('mhgd,khd->hgmk', grouped_heads, gathered_stretch_keys, prefer...  33.1 us
    dot_general x2, matrix products, block_stats(): jnp.einsum('hgmk,khd->mhgd', weights.astype(jnp.bfloat16), values, prefer...  29 us
    reduce_sum x2, other arithmetic, block_stats(): weight_sum = jnp.sum(weights, axis=-1)  22.9 us
    another operation x4, local copies, waits for them, and re-layouts  17.6 us
  transfers between devices with their start and end apart: 4, of which 4 were waited for; matrix products, arithmetic and copies ran while one was open for 25% of the time, Pallas kernels for 0%

commit v1 on v0

--- a/solution.py
+++ b/solution.py
@@ -1,6 +1,8 @@
 import jax
 import jax.numpy as jnp
 from jax import lax
+from jax.experimental import pallas as pl
+from jax.experimental.pallas import tpu as pltpu
 from jax.sharding import PartitionSpec as P
 
 STRETCH_TOKENS = 512
@@ -12,6 +14,133 @@
 eps_norm = 1e-06
 rope_base = 1000000.0
 floor_score = -1e30
+start_peak = -1e29
+LOG2E = 1.4426950408889634
+CHUNK = 128
+
+
+def held_kernel(slot_ref, place_ref, first_ref, q_ref, k_ref, v_ref, pos_ref, cos_ref, sin_ref,
+                o_ref, lse_ref, acc, peak, total):
+    req, rank = pl.program_id(0), pl.program_id(1)
+    ranks = pl.num_programs(1)
+    head = cos_ref.shape[1]
+    heads = k_ref.shape[2] // head
+    groups = q_ref.shape[2] // head // heads
+    chunks = q_ref.shape[1] // CHUNK
+    tokens = k_ref.shape[1]
+    scale = head ** (-0.5) * LOG2E
+
+    @pl.when(rank == 0)
+    def _():
+        acc[...] = jnp.zeros_like(acc)
+        peak[...] = jnp.full_like(peak, start_peak)
+        total[...] = jnp.zeros_like(total)
+
+    step = req * ranks + rank
+    place = place_ref[step]
+    first = first_ref[step]
+
+    @pl.when(first < chunks * CHUNK)
+    def _():
+        cosine = cos_ref[pl.ds(place, 1), :]
+        sine = sin_ref[pl.ds(place, 1), :]
+        rotated = []
+        for h in range(heads):
+            wide = k_ref[0, :, h * head:(h + 1) * head].astype(jnp.float32)
+            turned = pltpu.roll(wide, head // 2, 1)
+            rotated.append((wide * cosine + turned * sine).astype(jnp.bfloat16))
+        where_key = place * tokens + lax.broadcasted_iota(
+            jnp.int32, (tokens, groups * CHUNK), 0
+        )
+        for c in range(chunks):
+            @pl.when(first < (c + 1) * CHUNK)
+            def _():
+                row = pos_ref[0, :, c * CHUNK:(c + 1) * CHUNK]
+                live = where_key < jnp.concatenate([row] * groups, axis=1)
+                for h in range(heads):
+                    at = h * chunks + c
+                    query = jnp.concatenate(
+                        [
+                            q_ref[0, c * CHUNK:(c + 1) * CHUNK,
+                                  (h * groups + g) * head:(h * groups + g + 1) * head]
+                            for g in range(groups)
+                        ],
+                        axis=0,
+                    )
+                    scores = lax.dot_general(
+                        rotated[h], query, (((1,), (1,)), ((), ())),
+                        preferred_element_type=jnp.float32,
+                    )
+                    scores = jnp.where(live, scores * scale, floor_score)
+                    old = peak[at]
+                    new = jnp.maximum(old, jnp.max(scores, axis=0, keepdims=True))
+                    weights = jnp.exp2(scores - new)
+                    factor = jnp.exp2(old - new)
+                    peak[at] = new
+                    total[at] = total[at] * factor + jnp.sum(weights, axis=0, keepdims=True)
+                    acc[at] = acc[at] * factor + lax.dot_general(
+                        v_ref[0, :, h * head:(h + 1) * head], weights.astype(jnp.bfloat16),
+                        (((0,), (0,)), ((), ())), preferred_element_type=jnp.float32,
+                    )
+
+    @pl.when(rank == ranks - 1)
+    def _():
+        for h in range(heads):
+            for c in range(chunks):
+                at = h * chunks + c
+                some = total[at]
+                held = some > 0.0
+                safe = jnp.where(held, some, 1.0)
+                out = (acc[at] / safe).T.astype(o_ref.dtype)
+                for g in range(groups):
+                    o_ref[0, c * CHUNK:(c + 1) * CHUNK,
+                          (h * groups + g) * head:(h * groups + g + 1) * head] = out[
+                        g * CHUNK:(g + 1) * CHUNK]
+                lse_ref[0, at:at + 1, :] = jnp.where(held, peak[at] + jnp.log2(safe), start_peak)
+
+
+def held_attention(q_all, slots, places, firsts, key_pool, value_pool, positions, cosines, sines):
+    reqs, rows, width = q_all.shape
+    ranks = slots.shape[0] // reqs
+    tokens, kv_width = key_pool.shape[1:]
+    head = cosines.shape[1]
+    heads = kv_width // head
+    groups = width // kv_width
+    chunks = rows // CHUNK
+    pool = pl.BlockSpec((1, tokens, kv_width), lambda r, j, s, p, f: (s[r * ranks + j], 0, 0))
+    whole_table = pl.BlockSpec(cosines.shape, lambda r, j, s, p, f: (0, 0))
+    return pl.pallas_call(
+        held_kernel,
+        grid_spec=pltpu.PrefetchScalarGridSpec(
+            num_scalar_prefetch=3,
+            grid=(reqs, ranks),
+            in_specs=[
+                pl.BlockSpec((1, rows, width), lambda r, j, s, p, f: (r, 0, 0)),
+                pool,
+                pool,
+                pl.BlockSpec((1, 1, rows), lambda r, j, s, p, f: (r, 0, 0)),
+                whole_table,
+                whole_table,
+            ],
+            out_specs=[
+                pl.BlockSpec((1, rows, width), lambda r, j, s, p, f: (r, 0, 0)),
+                pl.BlockSpec((1, heads * chunks, groups * CHUNK), lambda r, j, s, p, f: (r, 0, 0)),
+            ],
+            scratch_shapes=[
+                pltpu.VMEM((heads * chunks, head, groups * CHUNK), jnp.float32),
+                pltpu.VMEM((heads * chunks, 1, groups * CHUNK), jnp.float32),
+                pltpu.VMEM((heads * chunks, 1, groups * CHUNK), jnp.float32),
+            ],
+        ),
+        out_shape=[
+            jax.ShapeDtypeStruct((reqs, rows, width), jnp.bfloat16),
+            jax.ShapeDtypeStruct((reqs, heads * chunks, groups * CHUNK), jnp.float32),
+        ],
+        compiler_params=pltpu.CompilerParams(
+            dimension_semantics=("arbitrary", "arbitrary"), vmem_limit_bytes=32 * 1024 * 1024
+        ),
+        name="held_attention",
+    )(slots, places, firsts, q_all, key_pool, value_pool, positions, cosines, sines)
 
 
 def norm_rows(matrix, gain_vec):
@@ -65,15 +194,6 @@
         row_peak.transpose(2, 0, 1).reshape(count_of_rows, head_total),
         weight_sum.transpose(2, 0, 1).reshape(count_of_rows, head_total),
     )
-
-
-def merge_stats(weighted, row_peak, weight_sum):
-    row_top = jnp.max(row_peak, axis=0)
-    factor = jnp.exp(row_peak - row_top[None])
-    merged = jnp.sum(weighted * factor[..., None], axis=0)
-    total_sum = jnp.sum(weight_sum * factor, axis=0)
-    result = (merged / total_sum[..., None]).astype(jnp.bfloat16)
-    return result.reshape(result.shape[0], -1)
 
 
 def swiglu(rows_in, w_gate, w_up):
@@ -143,58 +263,47 @@
         pair_rank[:, :, None] == jnp.arange(pair_cap)[None, None, :]
     )
     send_slot = jnp.sum(jnp.where(my_sends, slot_table[:, :, None], 0), axis=1)
-    send_keys = cached_key_pool[send_slot]
-    send_values = cached_value_pool[send_slot]
-    got_keys, got_values = (
-        lax.all_to_all(send_keys, "req", split_axis=0, concat_axis=0, tiled=True),
-        lax.all_to_all(send_values, "req", split_axis=0, concat_axis=0, tiled=True),
-    )
-    my_holder = lax.dynamic_index_in_dim(holder_table, my_index, 0, keepdims=False)
-    my_rank = lax.dynamic_index_in_dim(pair_rank, my_index, 0, keepdims=False)
-    buffer = my_holder * pair_cap + my_rank
-    position_shift_angle = angles(jnp.arange(MOST_STRETCHES) * STRETCH_TOKENS, head_size)[
-        None, :, None, None, :
-    ]
-    gathered_stretch_keys = got_keys.reshape((req_count * pair_cap,) + got_keys.shape[2:])[buffer]
-    gathered_stretch_keys = gathered_stretch_keys.reshape(
-        local_reqs, MOST_STRETCHES, STRETCH_TOKENS, key_heads, head_size
-    )
-    gathered_stretch_keys = rotate_halves(
-        gathered_stretch_keys.astype(jnp.float32), position_shift_angle
-    ).astype(jnp.bfloat16)
-    gathered_stretch_keys = gathered_stretch_keys.reshape(
-        local_reqs, MOST_STRETCHES * STRETCH_TOKENS, key_heads, head_size
-    )
-    gathered_stretch_values = got_values.reshape((req_count * pair_cap,) + got_values.shape[2:])[
-        buffer
-    ]
-    gathered_stretch_values = gathered_stretch_values.reshape(
-        local_reqs, MOST_STRETCHES * STRETCH_TOKENS, key_heads, head_size
-    )
-    key_place = jnp.arange(MOST_STRETCHES * STRETCH_TOKENS)
-
-    def cached_stats(packed):
-        group_query, position, length, key_block, value_block = packed
-        live_mask = (key_place[None, :] < position[:, None]) & (
-            key_place[None, :] // STRETCH_TOKENS < length
-        )
-        return block_stats(group_query, key_block, value_block, live_mask)
-
-    held_sum, held_peak, held_total = lax.map(
-        cached_stats,
-        (
-            grouped_heads.reshape(local_reqs, req_rows, key_heads, groups, head_size),
-            my_positions,
-            my_lengths,
-            gathered_stretch_keys,
-            gathered_stretch_values,
-        ),
-    )
-    attended = merge_stats(
-        jnp.stack([held_sum.reshape(fresh_sum.shape), fresh_sum]),
-        jnp.stack([held_peak.reshape(fresh_peak.shape), fresh_peak]),
-        jnp.stack([held_total.reshape(fresh_total.shape), fresh_total]),
-    )
+    place_ids = jnp.arange(MOST_STRETCHES)[None, :, None]
+    send_place = jnp.sum(jnp.where(my_sends, place_ids, 0), axis=1)
+    below = jnp.sum(
+        (recompute_pos[:, None, :] <= (send_place * STRETCH_TOKENS)[:, :, None]).astype(jnp.int32),
+        axis=2,
+    )
+    first_row = jnp.where(send_place < req_lengths[:, None], below, req_rows)
+    shift_angle = angles(jnp.arange(MOST_STRETCHES) * STRETCH_TOKENS, head_size)
+    cosine, sine = jnp.cos(shift_angle), jnp.sin(shift_angle)
+    queries_all = lax.all_gather(
+        queries.reshape(count_of_rows, query_heads * head_size), "req", axis=0
+    )
+    held_out, held_lse = held_attention(
+        queries_all,
+        send_slot.reshape(-1),
+        send_place.reshape(-1),
+        first_row.reshape(-1),
+        cached_key_pool,
+        cached_value_pool,
+        recompute_pos.reshape(req_count, 1, req_rows),
+        jnp.concatenate([cosine, cosine], axis=1),
+        jnp.concatenate([-sine, sine], axis=1),
+    )
+    got_out = lax.all_to_all(held_out, "req", split_axis=0, concat_axis=0, tiled=True)
+    got_lse = lax.all_to_all(held_lse, "req", split_axis=0, concat_axis=0, tiled=True)
+    chunks = req_rows // CHUNK
+    got_lse = (
+        got_lse.reshape(req_count, key_heads, chunks, groups, CHUNK)
+        .transpose(0, 2, 4, 1, 3)
+        .reshape(req_count, count_of_rows, query_heads)
+    )
+    row_top = jnp.maximum(jnp.max(got_lse, axis=0), fresh_peak * LOG2E)
+    held_factor = jnp.exp2(got_lse - row_top[None])
+    fresh_factor = jnp.exp2(fresh_peak * LOG2E - row_top)
+    weighted = fresh_sum * fresh_factor[..., None] + jnp.sum(
+        got_out.reshape(req_count, count_of_rows, query_heads, head_size).astype(jnp.float32)
+        * held_factor[..., None],
+        axis=0,
+    )
+    total = fresh_total * fresh_factor + jnp.sum(held_factor, axis=0)
+    attended = (weighted / total[..., None]).astype(jnp.bfloat16).reshape(count_of_rows, -1)
     attn_out = lax.psum(
         jnp.dot(attended, w_out, preferred_element_type=jnp.float32).astype(jnp.bfloat16), "tp"
     ).astype(jnp.float32)

time: 551 us -> 279 us (0.51)
  waiting for transfers between devices: 298 us -> 137 us
  matrix products: 86.6 us -> 27.2 us
  local copies, waits for them, and re-layouts: 85.4 us -> 33.5 us
  other arithmetic: 52 us -> 14 us
  Pallas kernels: 0 us -> 34.1 us
  blocking collectives: 0 us -> 10.9 us
    all_to_all x2 -> x1, waiting for transfers between devices: 225 us -> 22.7 us  [on_device(): lax.all_to_all(held_out, 'req', split_axis=0, concat_axis=0, tiled=True)]
    all_gather x0 -> x1, waiting for transfers between devices: none -> 41.4 us  [on_device(): lax.all_gather(queries.reshape(count_of_rows, query_heads * head_size), '...]
    pallas_call x0 -> x1, Pallas kernels: none -> 34.1 us  [held_attention(): pl.pallas_call(held_kernel, grid_spec=pltpu.PrefetchScalarGridSpec(num_sc...]
    gather x4 -> x0, local copies, waits for them, and re-layouts: 33.7 us -> none  [the longest x1 8.46 us: on_device(): got_values.reshape((req_count * pair_cap,) + got_values.shape[2:])[buffer]]
    dot_general x2 -> x1, matrix products: 33.1 us -> 1.45 us  [block_stats(): jnp.einsum('mhgd,khd->hgmk', grouped_heads, gathered_stretch_keys, prefer...]
    dot_general x2 -> x1, matrix products: 29 us -> 1.13 us  [block_stats(): jnp.einsum('hgmk,khd->mhgd', weights.astype(jnp.bfloat16), values, prefer...]
    reduce_sum x2 -> x1, other arithmetic: 22.9 us -> 0.21 us  [block_stats(): weight_sum = jnp.sum(weights, axis=-1)]
    another operation x7 -> x2, local copies, waits for them, and re-layouts: 18.9 us -> 2.41 us
  transfers between devices with their start and end apart: 4 -> 4, of which waited for: 4 -> 4; matrix products, arithmetic and copies ran while one was open for 25% -> 11% of each run, Pallas kernels for 0% -> 0%
where the time goes in v1:
time: 279 us
  waiting for transfers between devices  137 us (49%)
  Pallas kernels  34.1 us (12%)
  local copies, waits for them, and re-layouts  33.5 us (12%)
  matrix products  27.2 us (10%)
  other arithmetic  14 us (5%)
  between operations  13.6 us (5%)
  blocking collectives  10.9 us (4%)
  starting transfers between devices  8.18 us (3%)
    all_gather x1, waiting for transfers between devices, on_device(): lax.all_gather(queries.reshape(count_of_rows, query_heads * head_size), '...  41.4 us
    psum x1, waiting for transfers between devices, on_device(): lax.psum(jnp.dot(hidden, w_down, preferred_element_type=jnp.float32).asty...  36.6 us
    psum x1, waiting for transfers between devices, on_device(): lax.psum(jnp.dot(attended, w_out, preferred_element_type=jnp.float32).ast...  36.4 us
    pallas_call x1, Pallas kernels, held_attention(): pl.pallas_call(held_kernel, grid_spec=pltpu.PrefetchScalarGridSpec(num_sc...  34.1 us
    all_to_all x1, waiting for transfers between devices, on_device(): lax.all_to_all(held_out, 'req', split_axis=0, concat_axis=0, tiled=True)  22.7 us
    all_to_all x1, blocking collectives, on_device(): lax.all_to_all(held_lse, 'req', split_axis=0, concat_axis=0, tiled=True)  10.9 us
    unnamed x38, local copies, waits for them, and re-layouts  10.5 us
    dot_general x1, matrix products, on_device(): jnp.dot(hidden, w_down, preferred_element_type=jnp.float32)  9.57 us
  transfers between devices with their start and end apart: 4, of which 4 were waited for; matrix products, arithmetic and copies ran while one was open for 11% of the time, Pallas kernels for 0%

profile of v1, /device:TPU:29, one launch (start us, length us, event | category | flops | bytes accessed | tf_op | source)
XLA Modules:
  0.0 278.6 jit_solution(5464455923269974238)
XLA Ops:
  6.6 0.9 constant_dynamic-slice_fusion
  7.4 1.5 fusion.1
  8.9 2.7 fusion.38
  14.8 0.8 convert_element_type.96
  15.7 1.9 gather_fusion
  18.6 1.9 gather_fusion.1
  22.0 41.4 %all-gather.2.cloned.1.call-done.q_ref = bf16[8,256,512]{2,1,0:T(8,128)(2,1)} async-done(((bf16[1,256,512]{2,1,0:T(8,128)(2,1)}), bf16[8,256,512]{2,1,0:T(8,128)(2,1)}) %all-gather.2.cloned.1.call-update) | async-done | bytes 2097168 | tf_op jit(solution)/shard_map/all_gather | solution.py:275
  63.4 3.4 %copy-done.1 = bf16[32,512,256]{2,1,0:T(8,128)(2,1)S(1)} copy-done((bf16[32,512,256]{2,1,0:T(8,128)(2,1)S(1)}, bf16[32,512,256]{2,1,0:T(8,128)(2,1)}, u32[]{:S(2)}) %copy-start.1) | copy-done | bytes 8388632
  66.8 3.4 %copy-done.2 = bf16[32,512,256]{2,1,0:T(8,128)(2,1)S(1)} copy-done((bf16[32,512,256]{2,1,0:T(8,128)(2,1)S(1)}, bf16[32,512,256]{2,1,0:T(8,128)(2,1)}, u32[]{:S(2)}) %copy-start.2) | copy-done | bytes 8388632
  70.2 1.6 copy-done.4
  71.8 34.1 %held_attention.1 = (bf16[8,256,512]{2,1,0:T(8,128)(2,1)S(1)}, f32[8,4,256]{2,1,0:T(4,128)S(1)}) custom-call(s32[32]{0:T(128)S(1)} %reshape.262.slot_ref, s32[32]{0:T(128)S(1)} %reshape.263.place_ref, s32[32]{0:T(128)S(1)} %compare_select_fusion.1.first_ref, bf16[8,256,512]{2,1,0:T(8,128)(2,1)S(1)} %copy-done.4, bf16[32,512,256]{2,1,0:T(8,128)(2,1)S(1)} %copy-done.1, ...), custom_call_target="tpu_custom_call" | custom-call | tf_op jit(solution)/shard_map/held_attention/pallas_call | solution.py:112
  105.9 1.4 copy-done.3
  107.2 10.9 %all_to_all.10 = f32[8,4,256]{2,1,0:T(4,128)} all-to-all(f32[8,4,256]{2,1,0:T(4,128)S(1)} %get-tuple-element.7), channel_id=1, replica_groups=mesh['req'=8,'tp'=4] {'req'}, dimensions={0} | all-to-all | bytes 65536 | tf_op jit(solution)/shard_map/all_to_all | solution.py:290
  118.1 8.1 %all-to-all-start.1 = ((bf16[8,256,512]{2,1,0:T(8,128)(2,1)}), bf16[8,256,512]{2,1,0:T(8,128)(2,1)}, u32[]{:S(2)}, u32[]{:S(2)}) async-start(bf16[8,256,512]{2,1,0:T(8,128)(2,1)} %copy-done.3), calls=%async_computation.1 | async-start | bytes 4194304 | tf_op jit(solution)/shard_map/all_to_all | solution.py:289
  126.2 1.7 copy.76
  128.7 2.6 multiply_reduce_fusion.2
  131.3 1.1 copy.73
  132.9 1.5 select_reduce_fusion
  134.6 2.2 convolution_convert_fusion.2
  136.8 1.1 fusion.13
  137.9 2.1 copy.86
  140.6 3.8 %mul.333 = f32[8,256,4,128]{3,2,1,0:T(4,128)} broadcast(f32[8,256,4]{2,1,0:T(8,128)S(1)} %copy.87), dimensions={0,1,2} | broadcast | bytes 4227072 | tf_op jit(solution)/shard_map/mul | solution.py:301
  144.4 5.5 %mul.334 = f32[8,256,512]{2,1,0:T(8,128)} reshape(f32[8,256,4,128]{3,2,1,0:T(4,128)} %mul.333) | data formatting | bytes 8388608 | tf_op jit(solution)/shard_map/mul | solution.py:301
  150.2 22.7 %all-to-all-done.1 = bf16[8,256,512]{2,1,0:T(8,128)(2,1)} async-done(((bf16[8,256,512]{2,1,0:T(8,128)(2,1)}), bf16[8,256,512]{2,1,0:T(8,128)(2,1)}, u32[]{:S(2)}, u32[]{:S(2)}) %all-to-all-start.1) | async-done | bytes 2097184 | tf_op jit(solution)/shard_map/all_to_all | solution.py:289
  172.9 3.6 %multiply_reduce_fusion = f32[256,512]{1,0:T(8,128)S(1)} fusion(f32[8,256,512]{2,1,0:T(8,128)} %mul.334, bf16[8,256,512]{2,1,0:T(8,128)(2,1)} %all-to-all-done.1), kind=kLoop, calls=%fused_computation.2 | loop fusion | flops 3014656 | bytes 6815744 | tf_op jit(solution)/shard_map/reduce_sum | solution.py:300
  177.2 1.7 convolution_convert_fusion
  179.0 36.4 %all-reduce.3.cloned.1.call-done = bf16[256,2048]{1,0:T(8,128)(2,1)} async-done(((bf16[256,2048]{1,0:T(8,128)(2,1)}), bf16[256,2048]{1,0:T(8,128)(2,1)}) %all-reduce.3.cloned.1.call-update) | async-done | bytes 1048592 | tf_op jit(solution)/shard_map/psum | solution.py:307
  215.4 2.0 fusion.5
  217.5 5.8 %fusion.22 = f32[256,1536]{1,0:T(8,128)} fusion(bf16[2048,1536]{1,0:T(8,128)(2,1)} %param.33, bf16[256,2048]{1,0:T(8,128)(2,1)S(1)} %get-tuple-element.12, f32[2048]{0:T(1024)S(1)} %copy-done.18, f32[256]{0:T(256)S(1)} %add_rsqrt_fusion.2), kind=kOutput, calls=%fused_computation.42 | convolution fusion | flops 1612709888 | bytes 8922112 | tf_op jit(solution)/shard_map/dot_general | solution.py:200
  223.2 9.6 %convolution_convert_fusion.1 = bf16[256,2048]{1,0:T(8,128)(2,1)} fusion(bf16[1536,2048]{1,0:T(8,128)(2,1)} %param.35, bf16[2048,1536]{1,0:T(8,128)(2,1)} %param.34, f32[256,1536]{1,0:T(8,128)} %fusion.22, bf16[256,2048]{1,0:T(8,128)(2,1)S(1)} %get-tuple-element.12, f32[2048]{0:T(1024)S(1)} %copy-done.18, f32[256]{0:T(256)S(1)} %add_rsqrt_fusion.2), kind=kOutput, calls=%fused_computation.12 | convolution fusion | flops 3226206208 | bytes 16262144 | tf_op jit(solution)/shard_map/dot_general | solution.py:314
  232.8 36.6 %all-reduce.5.cloned.1.call-done = bf16[256,2048]{1,0:T(8,128)(2,1)} async-done(((bf16[256,2048]{1,0:T(8,128)(2,1)}), bf16[256,2048]{1,0:T(8,128)(2,1)}) %all-reduce.5.cloned.1.call-update) | async-done | bytes 1048592 | tf_op jit(solution)/shard_map/psum | solution.py:313
  269.5 2.6 fusion.8
  (101 shorter events, 8.6 us)
Async XLA Ops:
  6.5 170.6 %copy-start = (bf16[512,2048]{1,0:T(8,128)(2,1)S(1)}, bf16[512,2048]{1,0:T(8,128)(2,1)}, u32[]{:S(2)}) copy-start(bf16[512,2048]{1,0:T(8,128)(2,1)} %param.31) | copy-start | bytes 6291460
  6.5 56.9 %all-gather.2.cloned.1.call-start = ((), (), s32[]{:S(2)}) async-start(), calls=%async_computation.2 | async-start | bytes 2359296 | tf_op jit(solution)/shard_map/all_gather | solution.py:275
  11.6 1.1 copy-start.14
  12.8 2.8 %copy-start.8 = (f32[256,64]{1,0:T(8,128)}, f32[256,64]{1,0:T(8,128)S(1)}, u32[]{:S(2)}) copy-start(f32[256,64]{1,0:T(8,128)S(1)} %get-tuple-element.23) | copy-start | bytes 196612
  12.8 2.8 %copy-start.11 = (s32[8,256]{1,0:T(8,128)S(1)}, s32[8,256]{1,0:T(8,128)}, u32[]{:S(2)}) copy-start(s32[8,256]{1,0:T(8,128)} %param.19) | copy-start | bytes 24580
  12.8 2.8 %copy-start.12 = (s32[8,32]{1,0:T(8,128)S(1)}, s32[8,32]{1,0:T(8,128)}, u32[]{:S(2)}) copy-start(s32[8,32]{1,0:T(8,128)} %param.21) | copy-start | bytes 3076
  12.8 2.9 %copy-start.13 = (s32[2,256]{1,0:T(2,128)S(1)}, s32[2,256]{1,0:T(2,128)}, u32[]{:S(2)}) copy-start(s32[2,256]{1,0:T(2,128)} %param.22) | copy-start | bytes 6148
  13.7 0.7 copy-start.6
  18.6 2.8 %copy-start.16 = (s32[8]{0:T(128)S(1)}, s32[8]{0:T(128)}, u32[]{:S(2)}) copy-start(s32[8]{0:T(128)} %param.20) | copy-start | bytes 100
  63.4 3.4 %copy-start.1 = (bf16[32,512,256]{2,1,0:T(8,128)(2,1)S(1)}, bf16[32,512,256]{2,1,0:T(8,128)(2,1)}, u32[]{:S(2)}) copy-start(bf16[32,512,256]{2,1,0:T(8,128)(2,1)} %k_ref.1) | copy-start | bytes 25165828
  66.8 3.4 %copy-start.2 = (bf16[32,512,256]{2,1,0:T(8,128)(2,1)S(1)}, bf16[32,512,256]{2,1,0:T(8,128)(2,1)}, u32[]{:S(2)}) copy-start(bf16[32,512,256]{2,1,0:T(8,128)(2,1)} %v_ref.1) | copy-start | bytes 25165828
  70.2 1.6 copy-start.4
  105.8 1.4 copy-start.3
  118.1 10.6 %copy-start.5 = (bf16[256,2048]{1,0:T(8,128)(2,1)S(1)}, bf16[256,2048]{1,0:T(8,128)(2,1)}, u32[]{:S(2)}) copy-start(bf16[256,2048]{1,0:T(8,128)(2,1)} %param.18) | copy-start | bytes 3145732
  118.1 54.8 %all-to-all-start.1 = ((bf16[8,256,512]{2,1,0:T(8,128)(2,1)}), bf16[8,256,512]{2,1,0:T(8,128)(2,1)}, u32[]{:S(2)}, u32[]{:S(2)}) async-start(bf16[8,256,512]{2,1,0:T(8,128)(2,1)} %copy-done.3), calls=%async_computation.1 | async-start | bytes 4194304 | tf_op jit(solution)/shard_map/all_to_all | solution.py:289
  126.2 89.2 %all-reduce.3.cloned.1.call-start = ((), (), s32[]{:S(2)}) async-start(), calls=%async_computation.3 | async-start | bytes 2097152 | tf_op jit(solution)/shard_map/psum | solution.py:307
  127.9 4.6 %copy-start.15 = (f32[128]{0:T(128)S(1)}, f32[128]{0:T(128)}, u32[]{:S(2)}) copy-start(f32[128]{0:T(128)} %param.30) | copy-start | bytes 1540
  128.7 4.0 %copy-start.9 = (f32[256,64]{1,0:T(8,128)S(1)}, f32[256,64]{1,0:T(8,128)}, u32[]{:S(2)}) copy-start(f32[256,64]{1,0:T(8,128)} %copy-done.8) | copy-start | bytes 196612
  132.7 1.9 copy-start.17
  136.8 3.2 %copy-start.10 = (f32[8,4,256]{2,1,0:T(4,128)S(1)}, f32[8,4,256]{2,1,0:T(4,128)}, u32[]{:S(2)}) copy-start(f32[8,4,256]{2,1,0:T(4,128)} %all_to_all.10) | copy-start | bytes 98308
  150.2 27.0 %copy-start.7 = (f32[256,512]{1,0:T(8,128)S(1)}, f32[256,512]{1,0:T(8,128)}, u32[]{:S(2)}) copy-start(f32[256,512]{1,0:T(8,128)} %copy.86) | copy-start | bytes 1572868
  178.9 38.6 %copy-start.18 = (f32[2048]{0:T(1024)S(1)}, f32[2048]{0:T(1024)}, u32[]{:S(2)}) copy-start(f32[2048]{0:T(1024)} %param.32) | copy-start | bytes 24580
  178.9 90.6 %all-reduce.5.cloned.1.call-start = ((), (), s32[]{:S(2)}) async-start(), calls=%async_computation.4 | async-start | bytes 2097152 | tf_op jit(solution)/shard_map/psum | solution.py:313
Sparse Core Ops, SparseCore 0:
  15.7 47.6 all-gather.1
  179.0 36.3 all-reduce.2
  233.0 36.4 all-reduce.4

commit v2 on v1

--- a/solution.py
+++ b/solution.py
@@ -1,3 +1,5 @@
+import functools
+
 import jax
 import jax.numpy as jnp
 from jax import lax
@@ -17,6 +19,8 @@
 start_peak = -1e29
 LOG2E = 1.4426950408889634
 CHUNK = 128
+LSE_ROWS = 8
+MESH = pl.DeviceIdType.MESH
 
 
 def held_kernel(slot_ref, place_ref, first_ref, q_ref, k_ref, v_ref, pos_ref, cos_ref, sin_ref,
@@ -85,6 +89,7 @@
 
     @pl.when(rank == ranks - 1)
     def _():
+        lse_rows = []
         for h in range(heads):
             for c in range(chunks):
                 at = h * chunks + c
@@ -96,7 +101,10 @@
                     o_ref[0, c * CHUNK:(c + 1) * CHUNK,
                           (h * groups + g) * head:(h * groups + g + 1) * head] = out[
                         g * CHUNK:(g + 1) * CHUNK]
-                lse_ref[0, at:at + 1, :] = jnp.where(held, peak[at] + jnp.log2(safe), start_peak)
+                lse_rows.append(jnp.where(held, peak[at] + jnp.log2(safe), start_peak))
+        lse_ref[0] = jnp.concatenate(
+            lse_rows + [jnp.zeros_like(lse_rows[0])] * (LSE_ROWS - len(lse_rows)), axis=0
+        )
 
 
 def held_attention(q_all, slots, places, firsts, key_pool, value_pool, positions, cosines, sines):
@@ -124,7 +132,7 @@
             ],
             out_specs=[
                 pl.BlockSpec((1, rows, width), lambda r, j, s, p, f: (r, 0, 0)),
-                pl.BlockSpec((1, heads * chunks, groups * CHUNK), lambda r, j, s, p, f: (r, 0, 0)),
+                pl.BlockSpec((1, LSE_ROWS, groups * CHUNK), lambda r, j, s, p, f: (r, 0, 0)),
             ],
             scratch_shapes=[
                 pltpu.VMEM((heads * chunks, head, groups * CHUNK), jnp.float32),
@@ -134,7 +142,7 @@
         ),
         out_shape=[
             jax.ShapeDtypeStruct((reqs, rows, width), jnp.bfloat16),
-            jax.ShapeDtypeStruct((reqs, heads * chunks, groups * CHUNK), jnp.float32),
+            jax.ShapeDtypeStruct((reqs, LSE_ROWS, groups * CHUNK), jnp.float32),
         ],
         compiler_params=pltpu.CompilerParams(
             dimension_semantics=("arbitrary", "arbitrary"), vmem_limit_bytes=32 * 1024 * 1024
@@ -177,23 +185,243 @@
     return rotate_halves(normed, angles(position, head_size)[:, None, :]).astype(jnp.bfloat16)
 
 
-def block_stats(grouped_heads, gathered_stretch_keys, values, live_mask):
-    count_of_rows, key_heads, groups, head_size = grouped_heads.shape
-    scores = jnp.einsum(
-        "mhgd,khd->hgmk", grouped_heads, gathered_stretch_keys, preferred_element_type=jnp.float32
-    ) * head_size ** (-0.5)
-    row_peak = jnp.max(jnp.where(live_mask, scores, floor_score), axis=-1)
-    weights = jnp.where(live_mask, jnp.exp(scores - row_peak[..., None]), 0.0)
-    weight_sum = jnp.sum(weights, axis=-1)
-    weighted = jnp.einsum(
-        "hgmk,khd->mhgd", weights.astype(jnp.bfloat16), values, preferred_element_type=jnp.float32
-    )
-    head_total = key_heads * groups
-    return (
-        weighted.reshape(count_of_rows, head_total, head_size),
-        row_peak.transpose(2, 0, 1).reshape(count_of_rows, head_total),
-        weight_sum.transpose(2, 0, 1).reshape(count_of_rows, head_total),
-    )
+def merge_kernel(head, heads, groups, out_ref, lse_ref, q_ref, k_ref, v_ref, row_ref, col_ref,
+                 done_ref, got_out, got_lse, fresh_acc, fresh_peak, fresh_total, merged,
+                 send_out, recv_out, send_lse, recv_lse):
+    n = out_ref.shape[0]
+    me = lax.axis_index("req")
+    chunks = q_ref.shape[0] // CHUNK
+    scale = head ** (-0.5) * LOG2E
+
+    barrier = pltpu.get_barrier_semaphore()
+    for d in range(1, n):
+        pl.semaphore_signal(
+            barrier, inc=1, device_id={"req": lax.rem(me + d, n)}, device_id_type=MESH
+        )
+    pl.semaphore_wait(barrier, n - 1)
+
+    copies = []
+    for d in range(1, n):
+        other = lax.rem(me + d, n)
+        small = pltpu.make_async_remote_copy(
+            src_ref=lse_ref.at[other], dst_ref=got_lse.at[d - 1], send_sem=send_lse.at[d - 1],
+            recv_sem=recv_lse.at[d - 1], device_id={"req": other}, device_id_type=MESH,
+        )
+        small.start()
+        copies.append(small)
+    outs = []
+    for d in range(1, n):
+        other = lax.rem(me + d, n)
+        large = pltpu.make_async_remote_copy(
+            src_ref=out_ref.at[other], dst_ref=got_out.at[d - 1], send_sem=send_out.at[d - 1],
+            recv_sem=recv_out.at[d - 1], device_id={"req": other}, device_id_type=MESH,
+        )
+        large.start()
+        outs.append(large)
+
+    for c in range(chunks):
+        row = row_ref[:, c * CHUNK:(c + 1) * CHUNK]
+        live = col_ref[...] <= jnp.concatenate([row] * groups, axis=1)
+        for h in range(heads):
+            at = h * chunks + c
+            query = jnp.concatenate(
+                [
+                    q_ref[c * CHUNK:(c + 1) * CHUNK,
+                          (h * groups + g) * head:(h * groups + g + 1) * head]
+                    for g in range(groups)
+                ],
+                axis=0,
+            )
+            scores = lax.dot_general(
+                k_ref[:, h * head:(h + 1) * head], query, (((1,), (1,)), ((), ())),
+                preferred_element_type=jnp.float32,
+            )
+            scores = jnp.where(live, scores * scale, floor_score)
+            top = jnp.max(scores, axis=0, keepdims=True)
+            weights = jnp.exp2(scores - top)
+            fresh_peak[at] = top
+            fresh_total[at] = jnp.sum(weights, axis=0, keepdims=True)
+            fresh_acc[at] = lax.dot_general(
+                v_ref[:, h * head:(h + 1) * head], weights.astype(jnp.bfloat16),
+                (((0,), (0,)), ((), ())), preferred_element_type=jnp.float32,
+            )
+
+    for small in copies:
+        small.wait_recv()
+    own_lse = lse_ref[me]
+    columns = {}
+    for h in range(heads):
+        for c in range(chunks):
+            at = h * chunks + c
+            rows = [own_lse[at:at + 1, :]] + [got_lse[d - 1, at:at + 1, :] for d in range(1, n)]
+            top = fresh_peak[at]
+            for one in rows:
+                top = jnp.maximum(top, one)
+            fresh_factor = jnp.exp2(fresh_peak[at] - top)
+            factors = [jnp.exp2(one - top) for one in rows]
+            total = fresh_total[at] * fresh_factor
+            for one in factors:
+                total = total + one
+            inverse = 1.0 / total
+            stacked = jnp.concatenate(
+                [one * inverse for one in factors]
+                + [jnp.zeros((CHUNK - n, groups * CHUNK), jnp.float32)],
+                axis=0,
+            )
+            columns[at] = stacked.T
+            fresh = (fresh_acc[at] * (fresh_factor * inverse)).T
+            for g in range(groups):
+                at_rows = slice(c * CHUNK, (c + 1) * CHUNK)
+                at_cols = slice((h * groups + g) * head, (h * groups + g + 1) * head)
+                merged[at_rows, at_cols] = fresh[g * CHUNK:(g + 1) * CHUNK] + out_ref[
+                    me, at_rows, at_cols
+                ].astype(jnp.float32) * columns[at][g * CHUNK:(g + 1) * CHUNK, 0:1]
+    for d in range(1, n):
+        outs[d - 1].wait_recv()
+        for h in range(heads):
+            for c in range(chunks):
+                at = h * chunks + c
+                for g in range(groups):
+                    at_rows = slice(c * CHUNK, (c + 1) * CHUNK)
+                    at_cols = slice((h * groups + g) * head, (h * groups + g + 1) * head)
+                    merged[at_rows, at_cols] += got_out[d - 1, at_rows, at_cols].astype(
+                        jnp.float32
+                    ) * columns[at][g * CHUNK:(g + 1) * CHUNK, d:d + 1]
+    done_ref[...] = merged[...].astype(done_ref.dtype)
+    for copy in copies + outs:
+        copy.wait_send()
+
+
+def exchange_and_merge(held_out, held_lse, queries, keys, values, position, head):
+    n, rows, width = held_out.shape
+    heads = keys.shape[1] // head
+    groups = width // keys.shape[1]
+    pairs = heads * (rows // CHUNK)
+    vmem = pl.BlockSpec(memory_space=pltpu.VMEM)
+    return pl.pallas_call(
+        functools.partial(merge_kernel, head, heads, groups),
+        out_shape=jax.ShapeDtypeStruct((rows, width), jnp.bfloat16),
+        in_specs=[vmem] * 7,
+        out_specs=vmem,
+        scratch_shapes=[
+            pltpu.VMEM((n - 1, rows, width), jnp.bfloat16),
+            pltpu.VMEM((n - 1,) + held_lse.shape[1:], jnp.float32),
+            pltpu.VMEM((pairs, head, groups * CHUNK), jnp.float32),
+            pltpu.VMEM((pairs, 1, groups * CHUNK), jnp.float32),
+            pltpu.VMEM((pairs, 1, groups * CHUNK), jnp.float32),
+            pltpu.VMEM((rows, width), jnp.float32),
+        ]
+        + [pltpu.SemaphoreType.DMA((n - 1,))] * 4,
+        compiler_params=pltpu.CompilerParams(
+            collective_id=0, has_side_effects=True, vmem_limit_bytes=40 * 1024 * 1024
+        ),
+        name="exchange_and_merge",
+    )(held_out, held_lse, queries, keys, values, position[None, :], position[:, None])
+
+
+def group_sum_kernel(term_ref, base_ref, out_ref, pair_in, chip_sum, cross_in,
+                     send_pair, recv_pair, send_cross, recv_cross, send_own, recv_own,
+                     send_pass, recv_pass):
+    chips = chip_sum.shape[0]
+    rows = term_ref.shape[0]
+    half = rows // 2
+    part = half // chips
+    me = lax.axis_index("tp")
+    core = lax.rem(me, 2)
+    chip = me // 2
+    sibling = chip * 2 + 1 - core
+
+    def same_core(d):
+        return lax.rem(chip + d, chips)
+
+    def rows_of(core_at, chip_at):
+        return pl.ds(pl.multiple_of(core_at * half + chip_at * part, part), part)
+
+    barrier = pltpu.get_barrier_semaphore()
+    for d in range(1, chips):
+        pl.semaphore_signal(
+            barrier, inc=1, device_id={"tp": same_core(d) * 2 + core}, device_id_type=MESH
+        )
+    pl.semaphore_signal(barrier, inc=1, device_id={"tp": sibling}, device_id_type=MESH)
+    pl.semaphore_wait(barrier, chips)
+
+    order = list(range(1, chips)) + [0]
+    pair = {}
+    for d in order:
+        chip_at = same_core(d)
+        pair[d] = pltpu.make_async_remote_copy(
+            src_ref=term_ref.at[rows_of(1 - core, chip_at)], dst_ref=pair_in.at[d],
+            send_sem=send_pair.at[d], recv_sem=recv_pair.at[d],
+            device_id={"tp": sibling}, device_id_type=MESH,
+        )
+        pair[d].start()
+    cross = {}
+    for d in range(1, chips):
+        chip_at = same_core(d)
+        pair[d].wait_recv()
+        chip_sum[d] = (
+            term_ref[rows_of(core, chip_at), :].astype(jnp.float32)
+            + pair_in[d].astype(jnp.float32)
+        ).astype(chip_sum.dtype)
+        cross[d] = pltpu.make_async_remote_copy(
+            src_ref=chip_sum.at[d], dst_ref=cross_in.at[d],
+            send_sem=send_cross.at[d], recv_sem=recv_cross.at[d],
+            device_id={"tp": chip_at * 2 + core}, device_id_type=MESH,
+        )
+        cross[d].start()
+    pair[0].wait_recv()
+    mine = rows_of(core, chip)
+    summed = term_ref[mine, :].astype(jnp.float32) + pair_in[0].astype(jnp.float32)
+    for d in range(1, chips):
+        cross[d].wait_recv()
+        summed = summed + cross_in[d].astype(jnp.float32)
+    out_ref[mine, :] = (base_ref[mine, :].astype(jnp.float32) + summed).astype(out_ref.dtype)
+    own = []
+    for d in range(1, chips):
+        own.append(
+            pltpu.make_async_remote_copy(
+                src_ref=out_ref.at[mine], dst_ref=out_ref.at[mine],
+                send_sem=send_own.at[d], recv_sem=recv_own.at[d],
+                device_id={"tp": same_core(d) * 2 + core}, device_id_type=MESH,
+            )
+        )
+        own[-1].start()
+    passed = []
+    for d in range(chips):
+        if d > 0:
+            own[d - 1].wait_recv()
+        come = rows_of(core, lax.rem(chip - d + chips, chips))
+        passed.append(
+            pltpu.make_async_remote_copy(
+                src_ref=out_ref.at[come], dst_ref=out_ref.at[come],
+                send_sem=send_pass.at[d], recv_sem=recv_pass.at[d],
+                device_id={"tp": sibling}, device_id_type=MESH,
+            )
+        )
+        passed[-1].start()
+    for copy in passed:
+        copy.wait_recv()
+    for copy in list(pair.values()) + list(cross.values()) + own + passed:
+        copy.wait_send()
+
+
+def add_group_sum(term, base, collective_id):
+    chips = lax.axis_size("tp") // 2
+    rows, width = term.shape
+    part = rows // 2 // chips
+    vmem = pl.BlockSpec(memory_space=pltpu.VMEM)
+    return pl.pallas_call(
+        group_sum_kernel,
+        out_shape=jax.ShapeDtypeStruct((rows, width), jnp.bfloat16),
+        in_specs=[vmem] * 2,
+        out_specs=vmem,
+        scratch_shapes=[pltpu.VMEM((chips, part, width), jnp.bfloat16)] * 3
+        + [pltpu.SemaphoreType.DMA((chips,))] * 8,
+        compiler_params=pltpu.CompilerParams(
+            collective_id=collective_id, has_side_effects=True, vmem_limit_bytes=32 * 1024 * 1024
+        ),
+        name="add_group_sum",
+    )(term, base)
 
 
 def swiglu(rows_in, w_gate, w_up):
@@ -227,7 +455,6 @@
     head_size = query_gain.shape[0]
     query_heads = w_query.shape[1] // head_size
     key_heads = w_key.shape[1] // head_size
-    groups = query_heads // key_heads
     count_of_rows = hidden_in.shape[0]
     local_reqs = REQ_DEV
     req_rows = RECOMPUTE_TOKENS
@@ -239,21 +466,11 @@
     recomputed_values = (
         jnp.dot(normed, value_weight, preferred_element_type=jnp.float32)
         .astype(jnp.bfloat16)
-        .reshape(count_of_rows, key_heads, head_size)
     )
     my_positions = lax.dynamic_slice_in_dim(recompute_pos, my_index * local_reqs, local_reqs, 0)
-    my_lengths = lax.dynamic_slice_in_dim(req_lengths, my_index * local_reqs, local_reqs, 0)
     flattened_position = my_positions.reshape(count_of_rows)
     queries = rotary_heads(query_raw, query_gain, flattened_position, query_heads)
     recomputed_keys = rotary_heads(unnormed_keys, key_norm_gain, flattened_position, key_heads)
-    grouped_heads = queries.reshape(count_of_rows, key_heads, groups, head_size)
-    row_owner = jnp.arange(count_of_rows) // req_rows
-    own_mask = (row_owner[None, :] == row_owner[:, None]) & (
-        flattened_position[None, :] <= flattened_position[:, None]
-    )
-    fresh_sum, fresh_peak, fresh_total = block_stats(
-        grouped_heads, recomputed_keys, recomputed_values, own_mask
-    )
     holder_table = page_table[0][stretch_order]
     slot_table = page_table[1][stretch_order]
     holder_hits = holder_table[:, :, None] == jnp.arange(req_count)[None, None, :]
@@ -286,34 +503,21 @@
         jnp.concatenate([cosine, cosine], axis=1),
         jnp.concatenate([-sine, sine], axis=1),
     )
-    got_out = lax.all_to_all(held_out, "req", split_axis=0, concat_axis=0, tiled=True)
-    got_lse = lax.all_to_all(held_lse, "req", split_axis=0, concat_axis=0, tiled=True)
-    chunks = req_rows // CHUNK
-    got_lse = (
-        got_lse.reshape(req_count, key_heads, chunks, groups, CHUNK)
-        .transpose(0, 2, 4, 1, 3)
-        .reshape(req_count, count_of_rows, query_heads)
-    )
-    row_top = jnp.maximum(jnp.max(got_lse, axis=0), fresh_peak * LOG2E)
-    held_factor = jnp.exp2(got_lse - row_top[None])
-    fresh_factor = jnp.exp2(fresh_peak * LOG2E - row_top)
-    weighted = fresh_sum * fresh_factor[..., None] + jnp.sum(
-        got_out.reshape(req_count, count_of_rows, query_heads, head_size).astype(jnp.float32)
-        * held_factor[..., None],
-        axis=0,
-    )
-    total = fresh_total * fresh_factor + jnp.sum(held_factor, axis=0)
-    attended = (weighted / total[..., None]).astype(jnp.bfloat16).reshape(count_of_rows, -1)
-    attn_out = lax.psum(
-        jnp.dot(attended, w_out, preferred_element_type=jnp.float32).astype(jnp.bfloat16), "tp"
-    ).astype(jnp.float32)
-    residual = (hidden_in.astype(jnp.float32) + attn_out).astype(jnp.bfloat16)
+    attended = exchange_and_merge(
+        held_out,
+        held_lse,
+        queries.reshape(count_of_rows, query_heads * head_size),
+        recomputed_keys.reshape(count_of_rows, key_heads * head_size),
+        recomputed_values,
+        flattened_position,
+        head_size,
+    )
+    attn_term = jnp.dot(attended, w_out, preferred_element_type=jnp.float32).astype(jnp.bfloat16)
+    residual = add_group_sum(attn_term, hidden_in, 1)
     normed_ffn = norm_rows(residual, ffn_gain).astype(jnp.bfloat16)
     hidden = swiglu(normed_ffn, w_gate, w_up)
-    ffn_out = lax.psum(
-        jnp.dot(hidden, w_down, preferred_element_type=jnp.float32).astype(jnp.bfloat16), "tp"
-    ).astype(jnp.float32)
-    return (residual.astype(jnp.float32) + ffn_out).astype(jnp.bfloat16)
+    ffn_term = jnp.dot(hidden, w_down, preferred_element_type=jnp.float32).astype(jnp.bfloat16)
+    return add_group_sum(ffn_term, residual, 2)
 
 
 def solution(mesh):

time: 279 us -> 231 us (0.83)
  waiting for transfers between devices: 137 us -> 27.9 us
  Pallas kernels: 34.1 us -> 128 us
  blocking collectives: 10.9 us -> 0 us
  starting transfers between devices: 8.18 us -> 0.01 us
  local copies, waits for them, and re-layouts: 33.5 us -> 27.4 us
  other arithmetic: 14 us -> 9.4 us
  matrix products: 27.2 us -> 23.8 us
    pallas_call x0 -> x3, Pallas kernels: none -> 89.7 us  [the longest x1 50.6 us: exchange_and_merge(): pl.pallas_call(functools.partial(merge_kernel, head, heads, groups), out_...]
    psum x2 -> x0, waiting for transfers between devices: 73.1 us -> none  [the longest x1 36.6 us: on_device(): lax.psum(jnp.dot(hidden, w_down, preferred_element_type=jnp.float32).asty...]
    all_to_all x1 -> x0, waiting for transfers between devices: 22.7 us -> none  [on_device(): lax.all_to_all(held_out, 'req', split_axis=0, concat_axis=0, tiled=True)]
    all_gather x1, waiting for transfers between devices: 41.4 us -> 27.8 us  [on_device(): lax.all_gather(queries.reshape(count_of_rows, query_heads * head_size), '...]
    all_to_all x1 -> x0, blocking collectives: 10.9 us -> none  [on_device(): lax.all_to_all(held_lse, 'req', split_axis=0, concat_axis=0, tiled=True)]
    mul x5 -> x0, local copies, waits for them, and re-layouts: 9.65 us -> none  [the longest x2 9.29 us: on_device(): got_out.reshape(req_count, count_of_rows, query_heads, head_size)]
    all_to_all x1 -> x0, starting transfers between devices: 8.13 us -> none  [on_device(): lax.all_to_all(held_out, 'req', split_axis=0, concat_axis=0, tiled=True)]
    unnamed x38 -> x56, local copies, waits for them, and re-layouts: 10.5 us -> 15.5 us
  transfers between devices with their start and end apart: 4 -> 1, of which waited for: 4 -> 1; matrix products, arithmetic and copies ran while one was open for 11% -> 9% of each run, Pallas kernels for 0% -> 0%
where the time goes in v2:
time: 231 us; the launch traced here: 230 us
  Pallas kernels  128 us (55%)
  waiting for transfers between devices  27.9 us (12%)
  local copies, waits for them, and re-layouts  27.4 us (12%)
  matrix products  23.8 us (10%)
  between operations  13.8 us (6%)
  other arithmetic  9.4 us (4%)
    pallas_call x1, Pallas kernels, exchange_and_merge(): pl.pallas_call(functools.partial(merge_kernel, head, heads, groups), out_...  50.6 us
    pallas_call x2, Pallas kernels, add_group_sum(): pl.pallas_call(group_sum_kernel, out_shape=jax.ShapeDtypeStruct((rows, wi...  39.2 us
    pallas_call x1, Pallas kernels, held_attention(): pl.pallas_call(held_kernel, grid_spec=pltpu.PrefetchScalarGridSpec(num_sc...  37.8 us
    all_gather x1, waiting for transfers between devices, on_device(): lax.all_gather(queries.reshape(count_of_rows, query_heads * head_size), '...  27.8 us
    unnamed x56, local copies, waits for them, and re-layouts  15.5 us
    dot_general x1, matrix products, on_device(): jnp.dot(hidden, w_down, preferred_element_type=jnp.float32)  9.56 us
    dot_general x1, matrix products, swiglu(): gate_proj = jnp.dot(rows_in, w_gate, preferred_element_type=jnp.float32)  5.78 us
  transfers between devices with their start and end apart: 1, of which 1 were waited for; matrix products, arithmetic and copies ran while one was open for 9% of the time, Pallas kernels for 0%

profile of v2, /device:TPU:29, one launch (start us, length us, event | category | flops | bytes accessed | tf_op | source)
XLA Modules:
  0.0 229.9 jit_solution(4609852725124743628)
XLA Ops:
  6.6 0.9 fusion.22
  7.9 1.5 fusion.1
  9.5 3.5 %fusion.20 = f32[256,512]{1,0:T(8,128)} fusion(bf16[2048,512]{1,0:T(8,128)(2,1)} %param.26, bf16[256,2048]{1,0:T(8,128)(2,1)} %base_ref.1, f32[2048]{0:T(1024)} %param.25, f32[256]{0:T(256)S(1)} %add_rsqrt_fusion.3), kind=kOutput, calls=%fused_computation.60 | convolution fusion | flops 538968064 | bytes 3679232 | tf_op jit(solution)/shard_map/dot_general | solution.py:464
  13.0 1.2 reshape.152
  15.8 0.8 convert_element_type.83
  17.4 1.9 gather_fusion
  19.5 0.7 fusion.24
  20.3 1.9 gather_fusion.1
  22.6 0.7 reshape.151.place_ref
  25.7 1.0 copy.64
  26.8 1.9 multiply_reduce_fusion.1
  28.8 0.9 subtract_convert_fusion
  30.3 1.0 copy.60.k_ref
  31.4 0.8 copy.59.col_ref
  32.3 0.7 pad_maximum_fusion.1
  33.0 1.3 compare_select_fusion.1.first_ref
  34.3 2.4 %convolution_convert_fusion.2.v_ref = bf16[256,256]{1,0:T(8,128)(2,1)} fusion(bf16[2048,256]{1,0:T(8,128)(2,1)} %param.28, bf16[256,2048]{1,0:T(8,128)(2,1)S(1)} %copy-done.3, f32[2048]{0:T(1024)} %param.25, f32[256]{0:T(256)} %copy-done.21), kind=kOutput, calls=%fused_computation.16 | convolution fusion | flops 270598144 | bytes 2237440 | tf_op jit(solution)/shard_map/dot_general | solution.py:467
  36.6 27.8 %all-gather.2.cloned.1.call-done.q_ref = bf16[8,256,512]{2,1,0:T(8,128)(2,1)} async-done(((bf16[1,256,512]{2,1,0:T(8,128)(2,1)}), bf16[8,256,512]{2,1,0:T(8,128)(2,1)}) %all-gather.2.cloned.1.call-update) | async-done | bytes 2097168 | tf_op jit(solution)/shard_map/all_gather | solution.py:492
  64.5 3.4 %copy-done.1 = bf16[32,512,256]{2,1,0:T(8,128)(2,1)S(1)} copy-done((bf16[32,512,256]{2,1,0:T(8,128)(2,1)S(1)}, bf16[32,512,256]{2,1,0:T(8,128)(2,1)}, u32[]{:S(2)}) %copy-start.1) | copy-done | bytes 8388632
  67.9 3.4 %copy-done.2 = bf16[32,512,256]{2,1,0:T(8,128)(2,1)S(1)} copy-done((bf16[32,512,256]{2,1,0:T(8,128)(2,1)S(1)}, bf16[32,512,256]{2,1,0:T(8,128)(2,1)}, u32[]{:S(2)}) %copy-start.2) | copy-done | bytes 8388632
  71.2 1.6 copy-done.5
  72.8 0.7 copy-done.9
  73.6 0.7 copy-done.10
  76.3 37.8 %held_attention.1 = (bf16[8,256,512]{2,1,0:T(8,128)(2,1)S(1)}, f32[8,8,256]{2,1,0:T(8,128)S(1)}) custom-call(s32[32]{0:T(128)S(1)} %copy-done.14, s32[32]{0:T(128)S(1)} %copy-done.13, s32[32]{0:T(128)S(1)} %copy-done.15, bf16[8,256,512]{2,1,0:T(8,128)(2,1)S(1)} %copy-done.5, bf16[32,512,256]{2,1,0:T(8,128)(2,1)S(1)} %copy-done.1, ...), custom_call_target="tpu_custom_call" | custom-call | tf_op jit(solution)/shard_map/held_attention/pallas_call | solution.py:120
  114.1 50.6 %exchange_and_merge.1 = bf16[256,512]{1,0:T(8,128)(2,1)S(1)} custom-call(bf16[8,256,512]{2,1,0:T(8,128)(2,1)S(1)} %get-tuple-element.7.out_ref, f32[8,8,256]{2,1,0:T(8,128)S(1)} %get-tuple-element.8.lse_ref, bf16[256,512]{1,0:T(8,128)(2,1)S(1)} %bitcast.20, bf16[256,256]{1,0:T(8,128)(2,1)S(1)} %copy.60.k_ref, bf16[256,256]{1,0:T(8,128)(2,1)S(1)} %copy-done.8, ...), custom_call_target="tpu_custom_call" | custom-call | tf_op jit(solution)/shard_map/exchange_and_merge/pallas_call | solution.py:301
  164.8 0.7 convolution_convert_fusion.term_ref
  166.0 19.9 %add_group_sum.2.base_ref = bf16[256,2048]{1,0:T(8,128)(2,1)S(1)} custom-call(bf16[256,2048]{1,0:T(8,128)(2,1)S(1)} %convolution_convert_fusion.term_ref, bf16[256,2048]{1,0:T(8,128)(2,1)S(1)} %copy-done.4), custom_call_target="tpu_custom_call" | custom-call | tf_op jit(solution)/shard_map/add_group_sum/pallas_call | solution.py:413
  186.2 5.8 %fusion.10 = f32[256,1536]{1,0:T(8,128)} fusion(bf16[2048,1536]{1,0:T(8,128)(2,1)} %param.33, bf16[256,2048]{1,0:T(8,128)(2,1)S(1)} %add_group_sum.2.base_ref, f32[2048]{0:T(1024)S(1)} %copy-done.26, f32[256]{0:T(256)S(1)} %add_rsqrt_fusion.2), kind=kOutput, calls=%fused_computation.24 | convolution fusion | flops 1612709888 | bytes 8922112 | tf_op jit(solution)/shard_map/dot_general | solution.py:428
  192.0 9.6 %convolution_convert_fusion.1.term_ref = bf16[256,2048]{1,0:T(8,128)(2,1)} fusion(bf16[1536,2048]{1,0:T(8,128)(2,1)} %param.35, bf16[2048,1536]{1,0:T(8,128)(2,1)} %param.34, f32[256,1536]{1,0:T(8,128)} %fusion.10, bf16[256,2048]{1,0:T(8,128)(2,1)S(1)} %add_group_sum.2.base_ref, f32[2048]{0:T(1024)S(1)} %copy-done.26, f32[256]{0:T(256)S(1)} %add_rsqrt_fusion.2), kind=kOutput, calls=%fused_computation.9 | convolution fusion | flops 3226206208 | bytes 16262144 | tf_op jit(solution)/shard_map/dot_general | solution.py:519
  201.5 1.2 copy-done.6
  202.8 19.3 %add_group_sum.3 = bf16[256,2048]{1,0:T(8,128)(2,1)S(1)} custom-call(bf16[256,2048]{1,0:T(8,128)(2,1)S(1)} %copy-done.6, bf16[256,2048]{1,0:T(8,128)(2,1)S(1)} %add_group_sum.2.base_ref), custom_call_target="tpu_custom_call" | custom-call | tf_op jit(solution)/shard_map/add_group_sum/pallas_call | solution.py:413
  222.0 1.0 copy.66
  (87 shorter events, 9.6 us)
Async XLA Ops:
  6.5 158.2 %copy-start = (bf16[512,2048]{1,0:T(8,128)(2,1)S(1)}, bf16[512,2048]{1,0:T(8,128)(2,1)}, u32[]{:S(2)}) copy-start(bf16[512,2048]{1,0:T(8,128)(2,1)} %param.31) | copy-start | bytes 6291460
  6.5 57.9 %all-gather.2.cloned.1.call-start = ((), (), s32[]{:S(2)}) async-start(), calls=%async_computation | async-start | bytes 2359296 | tf_op jit(solution)/shard_map/all_gather | solution.py:492
  7.4 23.9 %copy-start.11 = (s32[1,256]{1,0:T(1,128)}, s32[1,256]{1,0:T(1,128)S(1)}, u32[]{:S(2)}) copy-start(s32[1,256]{1,0:T(1,128)S(1)} %get-tuple-element.12.row_ref) | copy-start | bytes 3076
  7.7 6.8 %copy-start.17 = (f32[256,64]{0,1:T(8,128)}, f32[256,64]{0,1:T(8,128)S(1)}, u32[]{:S(2)}) copy-start(f32[256,64]{0,1:T(8,128)S(1)} %get-tuple-element.20) | copy-start | bytes 196612
  9.5 17.3 %copy-start.21 = (f32[256]{0:T(256)}, f32[256]{0:T(256)S(1)}, u32[]{:S(2)}) copy-start(f32[256]{0:T(256)S(1)} %add_rsqrt_fusion.3) | copy-start | bytes 3076
  9.5 5.1 %copy-start.22 = (f32[128]{0:T(128)S(1)}, f32[128]{0:T(128)}, u32[]{:S(2)}) copy-start(f32[128]{0:T(128)} %param.29) | copy-start | bytes 1540
  14.6 2.1 copy-start.18
  14.6 2.7 %copy-start.19 = (s32[8,32]{1,0:T(8,128)S(1)}, s32[8,32]{1,0:T(8,128)}, u32[]{:S(2)}) copy-start(s32[8,32]{1,0:T(8,128)} %param.21) | copy-start | bytes 3076
  14.6 2.7 %copy-start.20 = (s32[2,256]{1,0:T(2,128)S(1)}, s32[2,256]{1,0:T(2,128)}, u32[]{:S(2)}) copy-start(s32[2,256]{1,0:T(2,128)} %param.22) | copy-start | bytes 6148
  15.8 9.9 %copy-start.16 = (bf16[256,4,128]{2,1,0:T(4,128)(2,1)}, bf16[256,4,128]{2,1,0:T(4,128)(2,1)S(1)}, u32[]{:S(2)}) copy-start(bf16[256,4,128]{2,1,0:T(4,128)(2,1)S(1)} %maximum_convert_fusion) | copy-start | bytes 786436
  20.2 4.0 %copy-start.24 = (s32[8]{0:T(128)S(1)}, s32[8]{0:T(128)}, u32[]{:S(2)}) copy-start(s32[8]{0:T(128)} %param.20) | copy-start | bytes 100
  20.2 6.5 %copy-start.3 = (bf16[256,2048]{1,0:T(8,128)(2,1)S(1)}, bf16[256,2048]{1,0:T(8,128)(2,1)}, u32[]{:S(2)}) copy-start(bf16[256,2048]{1,0:T(8,128)(2,1)} %base_ref.1) | copy-start | bytes 3145732
  20.2 6.5 %copy-start.25 = (f32[2048]{0:T(1024)S(1)}, f32[2048]{0:T(1024)}, u32[]{:S(2)}) copy-start(f32[2048]{0:T(1024)} %param.25) | copy-start | bytes 24580
  22.2 6.5 %copy-start.23 = (f32[128]{0:T(128)S(1)}, f32[128]{0:T(128)}, u32[]{:S(2)}) copy-start(f32[128]{0:T(128)} %param.30) | copy-start | bytes 1540
  64.5 3.4 %copy-start.1 = (bf16[32,512,256]{2,1,0:T(8,128)(2,1)S(1)}, bf16[32,512,256]{2,1,0:T(8,128)(2,1)}, u32[]{:S(2)}) copy-start(bf16[32,512,256]{2,1,0:T(8,128)(2,1)} %k_ref.1) | copy-start | bytes 25165828
  67.9 3.4 %copy-start.2 = (bf16[32,512,256]{2,1,0:T(8,128)(2,1)S(1)}, bf16[32,512,256]{2,1,0:T(8,128)(2,1)}, u32[]{:S(2)}) copy-start(bf16[32,512,256]{2,1,0:T(8,128)(2,1)} %v_ref.1) | copy-start | bytes 25165828
  71.2 1.6 copy-start.5
  72.8 0.7 copy-start.9
  73.6 0.7 copy-start.10
  74.3 0.7 copy-start.13
  74.9 0.7 copy-start.14
  75.6 0.7 copy-start.15
  76.3 37.9 %copy-start.7 = (s32[256,1]{1,0:T(8,128)S(1)}, s32[256,1]{1,0:T(8,128)}, u32[]{:S(2)}) copy-start(s32[256,1]{1,0:T(8,128)} %copy.59.col_ref) | copy-start | bytes 3076
  76.3 37.9 %copy-start.8 = (bf16[256,256]{1,0:T(8,128)(2,1)S(1)}, bf16[256,256]{1,0:T(8,128)(2,1)}, u32[]{:S(2)}) copy-start(bf16[256,256]{1,0:T(8,128)(2,1)} %convolution_convert_fusion.2.v_ref) | copy-start | bytes 393220
  76.3 37.9 %copy-start.12 = (s32[1,256]{1,0:T(1,128)S(1)}, s32[1,256]{1,0:T(1,128)}, u32[]{:S(2)}) copy-start(s32[1,256]{1,0:T(1,128)} %copy-done.11) | copy-start | bytes 3076
  164.7 1.2 copy-start.4
  166.0 20.2 %copy-start.26 = (f32[2048]{0:T(1024)S(1)}, f32[2048]{0:T(1024)}, u32[]{:S(2)}) copy-start(f32[2048]{0:T(1024)} %param.32) | copy-start | bytes 24580
  201.5 1.2 copy-start.6
Sparse Core Ops, SparseCore 0:
  16.8 47.6 all-gather.1

commit v3 on v2

--- a/solution.py
+++ b/solution.py
@@ -145,7 +145,7 @@
             jax.ShapeDtypeStruct((reqs, LSE_ROWS, groups * CHUNK), jnp.float32),
         ],
         compiler_params=pltpu.CompilerParams(
-            dimension_semantics=("arbitrary", "arbitrary"), vmem_limit_bytes=32 * 1024 * 1024
+            dimension_semantics=("arbitrary", "arbitrary"), vmem_limit_bytes=56 * 1024 * 1024
         ),
         name="held_attention",
     )(slots, places, firsts, q_all, key_pool, value_pool, positions, cosines, sines)

time: 231 us -> 231 us (level)
  local copies, waits for them, and re-layouts: 27.4 us -> 15.8 us
  Pallas kernels: 128 us -> 139 us
    unnamed x56 -> x36, local copies, waits for them, and re-layouts: 15.5 us -> 6.15 us
    pallas_call x1, Pallas kernels: 37.8 us -> 46.4 us  [held_attention(): pl.pallas_call(held_kernel, grid_spec=pltpu.PrefetchScalarGridSpec(num_sc...]
  transfers between devices with their start and end apart: 1 -> 1, of which waited for: 1 -> 1; matrix products, arithmetic and copies ran while one was open for 9% -> 8% of each run, Pallas kernels for 0% -> 0%
where the time goes in v3:
time: 231 us; the launch traced here: 230 us
  Pallas kernels  139 us (60%)
  waiting for transfers between devices  29.2 us (13%)
  matrix products  23.2 us (10%)
  local copies, waits for them, and re-layouts  15.8 us (7%)
  between operations  13.7 us (6%)
  other arithmetic  9.25 us (4%)
    pallas_call x1, Pallas kernels, exchange_and_merge(): pl.pallas_call(functools.partial(merge_kernel, head, heads, groups), out_...  52.2 us
    pallas_call x1, Pallas kernels, held_attention(): pl.pallas_call(held_kernel, grid_spec=pltpu.PrefetchScalarGridSpec(num_sc...  46.4 us
    pallas_call x2, Pallas kernels, add_group_sum(): pl.pallas_call(group_sum_kernel, out_shape=jax.ShapeDtypeStruct((rows, wi...  40 us
    all_gather x1, waiting for transfers between devices, on_device(): lax.all_gather(queries.reshape(count_of_rows, query_heads * head_size), '...  29.2 us
    dot_general x1, matrix products, on_device(): jnp.dot(hidden, w_down, preferred_element_type=jnp.float32)  9.58 us
    unnamed x36, local copies, waits for them, and re-layouts  6.15 us
    dot_general x1, matrix products, swiglu(): gate_proj = jnp.dot(rows_in, w_gate, preferred_element_type=jnp.float32)  5.8 us
  transfers between devices with their start and end apart: 1, of which 1 were waited for; matrix products, arithmetic and copies ran while one was open for 8% of the time, Pallas kernels for 0%

profile of v3, /device:TPU:29, one launch (start us, length us, event | category | flops | bytes accessed | tf_op | source)
XLA Modules:
  0.0 229.8 jit_solution(17846249142427918588)
XLA Ops:
  6.6 0.9 fusion.22
  7.9 1.5 fusion.1
  9.5 2.7 %fusion.20 = f32[256,512]{1,0:T(8,128)S(1)} fusion(bf16[2048,512]{1,0:T(8,128)(2,1)} %param.26, bf16[256,2048]{1,0:T(8,128)(2,1)} %base_ref.1, f32[2048]{0:T(1024)} %param.25, f32[256]{0:T(256)S(1)} %add_rsqrt_fusion.3), kind=kOutput, calls=%fused_computation.60 | convolution fusion | flops 538968064 | bytes 3679232 | tf_op jit(solution)/shard_map/dot_general | solution.py:464
  13.1 0.5 multiply_subtract_fusion
  14.0 0.8 convert_element_type.83
  14.9 0.6 broadcast_in_dim.39.pos_ref
  15.6 1.9 gather_fusion
  17.7 0.7 fusion.24
  18.5 2.0 gather_fusion.1
  21.4 0.7 lt.20
  22.2 0.6 reshape.150.slot_ref
  22.8 1.0 copy.64
  23.8 2.0 multiply_reduce_fusion.1
  25.8 0.7 multiply_multiply_fusion.1
  26.5 0.7 pad_maximum_fusion
  27.2 1.0 copy.60.k_ref
  28.2 0.8 copy.59.col_ref
  29.2 0.7 pad_maximum_fusion.1
  29.8 1.2 compare_select_fusion.1.first_ref
  31.1 2.4 %convolution_convert_fusion.2.v_ref = bf16[256,256]{1,0:T(8,128)(2,1)} fusion(bf16[2048,256]{1,0:T(8,128)(2,1)} %param.28, bf16[256,2048]{1,0:T(8,128)(2,1)S(1)} %copy-done.1, f32[2048]{0:T(1024)} %param.25, f32[256]{0:T(256)} %copy-done.13), kind=kOutput, calls=%fused_computation.16 | convolution fusion | flops 270598144 | bytes 2237440 | tf_op jit(solution)/shard_map/dot_general | solution.py:467
  33.5 29.2 %all-gather.2.cloned.1.call-done.q_ref = bf16[8,256,512]{2,1,0:T(8,128)(2,1)} async-done(((bf16[1,256,512]{2,1,0:T(8,128)(2,1)}), bf16[8,256,512]{2,1,0:T(8,128)(2,1)}) %all-gather.2.cloned.1.call-update) | async-done | bytes 2097168 | tf_op jit(solution)/shard_map/all_gather | solution.py:492
  62.7 46.4 %held_attention.1 = (bf16[8,256,512]{2,1,0:T(8,128)(2,1)}, f32[8,8,256]{2,1,0:T(8,128)}) custom-call(s32[32]{0:T(128)} %reshape.150.slot_ref, s32[32]{0:T(128)} %copy-done.10, s32[32]{0:T(128)} %compare_select_fusion.1.first_ref, bf16[8,256,512]{2,1,0:T(8,128)(2,1)} %all-gather.2.cloned.1.call-done.q_ref, bf16[32,512,256]{2,1,0:T(8,128)(2,1)} %k_ref.1, ...), custom_call_target="tpu_custom_call" | custom-call | tf_op jit(solution)/shard_map/held_attention/pallas_call | solution.py:120
  109.2 1.6 copy-done.3
  110.8 0.8 copy-done.7
  111.6 52.2 %exchange_and_merge.1 = bf16[256,512]{1,0:T(8,128)(2,1)S(1)} custom-call(bf16[8,256,512]{2,1,0:T(8,128)(2,1)S(1)} %copy-done.3, f32[8,8,256]{2,1,0:T(8,128)S(1)} %copy-done.7, bf16[256,512]{1,0:T(8,128)(2,1)S(1)} %bitcast.20, bf16[256,256]{1,0:T(8,128)(2,1)S(1)} %copy.60.k_ref, bf16[256,256]{1,0:T(8,128)(2,1)S(1)} %copy-done.6, ...), custom_call_target="tpu_custom_call" | custom-call | tf_op jit(solution)/shard_map/exchange_and_merge/pallas_call | solution.py:301
  163.8 0.7 convolution_convert_fusion.term_ref
  165.0 20.7 %add_group_sum.2.base_ref = bf16[256,2048]{1,0:T(8,128)(2,1)S(1)} custom-call(bf16[256,2048]{1,0:T(8,128)(2,1)S(1)} %convolution_convert_fusion.term_ref, bf16[256,2048]{1,0:T(8,128)(2,1)S(1)} %copy-done.2), custom_call_target="tpu_custom_call" | custom-call | tf_op jit(solution)/shard_map/add_group_sum/pallas_call | solution.py:413
  186.0 5.8 %fusion.10 = f32[256,1536]{1,0:T(8,128)} fusion(bf16[2048,1536]{1,0:T(8,128)(2,1)} %param.33, bf16[256,2048]{1,0:T(8,128)(2,1)S(1)} %add_group_sum.2.base_ref, f32[2048]{0:T(1024)S(1)} %copy-done.16, f32[256]{0:T(256)S(1)} %add_rsqrt_fusion.2), kind=kOutput, calls=%fused_computation.24 | convolution fusion | flops 1612709888 | bytes 8922112 | tf_op jit(solution)/shard_map/dot_general | solution.py:428
  191.8 9.6 %convolution_convert_fusion.1.term_ref = bf16[256,2048]{1,0:T(8,128)(2,1)} fusion(bf16[1536,2048]{1,0:T(8,128)(2,1)} %param.35, bf16[2048,1536]{1,0:T(8,128)(2,1)} %param.34, f32[256,1536]{1,0:T(8,128)} %fusion.10, bf16[256,2048]{1,0:T(8,128)(2,1)S(1)} %add_group_sum.2.base_ref, f32[2048]{0:T(1024)S(1)} %copy-done.16, f32[256]{0:T(256)S(1)} %add_rsqrt_fusion.2), kind=kOutput, calls=%fused_computation.9 | convolution fusion | flops 3226206208 | bytes 16262144 | tf_op jit(solution)/shard_map/dot_general | solution.py:519
  201.4 1.2 copy-done.4
  202.6 19.3 %add_group_sum.3 = bf16[256,2048]{1,0:T(8,128)(2,1)S(1)} custom-call(bf16[256,2048]{1,0:T(8,128)(2,1)S(1)} %copy-done.4, bf16[256,2048]{1,0:T(8,128)(2,1)S(1)} %add_group_sum.2.base_ref), custom_call_target="tpu_custom_call" | custom-call | tf_op jit(solution)/shard_map/add_group_sum/pallas_call | solution.py:413
  222.0 1.0 copy.66
  (67 shorter events, 4.1 us)
Async XLA Ops:
  6.5 157.2 %copy-start = (bf16[512,2048]{1,0:T(8,128)(2,1)S(1)}, bf16[512,2048]{1,0:T(8,128)(2,1)}, u32[]{:S(2)}) copy-start(bf16[512,2048]{1,0:T(8,128)(2,1)} %param.31) | copy-start | bytes 6291460
  6.5 56.2 %all-gather.2.cloned.1.call-start = ((), (), s32[]{:S(2)}) async-start(), calls=%async_computation | async-start | bytes 2359296 | tf_op jit(solution)/shard_map/all_gather | solution.py:492
  9.4 8.1 %copy-start.13 = (f32[256]{0:T(256)}, f32[256]{0:T(256)S(1)}, u32[]{:S(2)}) copy-start(f32[256]{0:T(256)S(1)} %add_rsqrt_fusion.3) | copy-start | bytes 3076
  9.5 3.3 %copy-start.14 = (f32[128]{0:T(128)S(1)}, f32[128]{0:T(128)}, u32[]{:S(2)}) copy-start(f32[128]{0:T(128)} %param.29) | copy-start | bytes 1540
  12.7 2.1 copy-start.9
  12.8 2.7 %copy-start.11 = (s32[8,32]{1,0:T(8,128)S(1)}, s32[8,32]{1,0:T(8,128)}, u32[]{:S(2)}) copy-start(s32[8,32]{1,0:T(8,128)} %param.21) | copy-start | bytes 3076
  12.8 2.8 %copy-start.12 = (s32[2,256]{1,0:T(2,128)S(1)}, s32[2,256]{1,0:T(2,128)}, u32[]{:S(2)}) copy-start(s32[2,256]{1,0:T(2,128)} %param.22) | copy-start | bytes 6148
  14.0 3.6 %copy-start.8 = (bf16[256,4,128]{2,1,0:T(4,128)(2,1)}, bf16[256,4,128]{2,1,0:T(4,128)(2,1)S(1)}, u32[]{:S(2)}) copy-start(bf16[256,4,128]{2,1,0:T(4,128)(2,1)S(1)} %maximum_convert_fusion) | copy-start | bytes 786436
  18.5 2.8 %copy-start.15 = (s32[8]{0:T(128)S(1)}, s32[8]{0:T(128)}, u32[]{:S(2)}) copy-start(s32[8]{0:T(128)} %param.20) | copy-start | bytes 100
  18.5 5.2 %copy-start.1 = (bf16[256,2048]{1,0:T(8,128)(2,1)S(1)}, bf16[256,2048]{1,0:T(8,128)(2,1)}, u32[]{:S(2)}) copy-start(bf16[256,2048]{1,0:T(8,128)(2,1)} %base_ref.1) | copy-start | bytes 3145732
  20.9 8.9 %copy-start.10 = (s32[32]{0:T(128)}, s32[32]{0:T(128)S(1)}, u32[]{:S(2)}) copy-start(s32[32]{0:T(128)S(1)} %reshape.151.place_ref) | copy-start | bytes 388
  62.7 46.4 %copy-start.5 = (s32[256,1]{1,0:T(8,128)S(1)}, s32[256,1]{1,0:T(8,128)}, u32[]{:S(2)}) copy-start(s32[256,1]{1,0:T(8,128)} %copy.59.col_ref) | copy-start | bytes 3076
  62.7 46.4 %copy-start.6 = (bf16[256,256]{1,0:T(8,128)(2,1)S(1)}, bf16[256,256]{1,0:T(8,128)(2,1)}, u32[]{:S(2)}) copy-start(bf16[256,256]{1,0:T(8,128)(2,1)} %convolution_convert_fusion.2.v_ref) | copy-start | bytes 393220
  109.2 1.6 copy-start.3
  110.8 0.8 copy-start.7
  163.8 1.2 copy-start.2
  165.0 21.0 %copy-start.16 = (f32[2048]{0:T(1024)S(1)}, f32[2048]{0:T(1024)}, u32[]{:S(2)}) copy-start(f32[2048]{0:T(1024)} %param.32) | copy-start | bytes 24580
  201.4 1.2 copy-start.4
Sparse Core Ops, SparseCore 0:
  15.0 47.6 all-gather.1
